TPU v7x, 32 devices: a whole 2x2x4 slice. The times are simulated.
32 devices in a mesh: fsdp: 8 (over y, x, core), tp: 4 (over z).
Axes of the slice: x: 2, y: 2, z: 4, core: 2. Of those that a mesh axis runs over, the one named last changes fastest.
Arguments:
- dec_queries: bfloat16 [2, 16, 8192], P(None, 'fsdp', 'tp'), may hold values from -160 to 160
- cache_keys: bfloat16 [16, 4096, 1024], P('fsdp', None, 'tp'), may hold values from -5.2 to 5.2
- cached_value_rows: bfloat16 [16, 4096, 1024], P('fsdp', None, 'tp'), may hold values from -6 to 6
- step_keys: bfloat16 [2, 16, 1024], P(None, 'fsdp', 'tp'), may hold values from -6 to 6
- step_values: bfloat16 [2, 16, 1024], P(None, 'fsdp', 'tp'), may hold values from -6 to 6
- prompt_lengths: int32 [16], P('fsdp'), may hold values from 2 to 4096
- resp_embed: bfloat16 [128, 32, 8192], P('fsdp', None, 'tp'), may hold values from -520 to 520
- resp_ids: int32 [128, 32], P('fsdp'), may hold values from 0 to 152063
- resp_lengths: int32 [128], P('fsdp'), may hold values from 25 to 32
- dest_shard: int32 [128], P('fsdp'), may hold values from 0 to 7, as said below
- dest_offset: int32 [128], P('fsdp'), may hold values from 0 to 511, as said below
- norm_gain: float32 [8192], replicated, may hold values from 0.7 to 7
- w_q: bfloat16 [8192, 8192], P('fsdp', 'tp'), may hold values from -0.0625 to 0.0625
- key_value_weight: bfloat16 [8192, 2, 1024], P('fsdp', None, 'tp'), may hold values from -0.0625 to 0.0625
- bias_q: float32 [8192], P('tp'), may hold values from -3 to 3
- key_value_bias: float32 [2, 1024], P(None, 'tp'), may hold values from -3 to 3
Outputs:
- decode_out: bfloat16 [2, 16, 8192], P(None, 'fsdp', 'tp')
- packed_ids: int32 [4096], P('fsdp')
- ref_attn: bfloat16 [4096, 8192], P('fsdp', 'tp')
Inputs may be any that keep to these rules, and one draw needn't show every extreme that they name: `dest_shard`: each shard receives exactly 16 responses; the 16 responses held by one index of fsdp go 4 each to half of the shards and none to the others. The responses of one shard occupy disjoint runs from dest_offset to dest_offset + resp_lengths - 1 within its 512 positions.
All inputs are finite; a program needn't handle non-finite values.
Results may differ from a plain program's by a relative error of at most 0.005.
The roundings to bfloat16 on the way count: a program that leaves them out, or rounds other values in their place, can miss the bound.
Values may be sent and summed in bfloat16 or wider, within the bound.
A program may use at most 128 MiB of HBM per device.

v0:
```python
import jax
import jax.numpy as jnp
from jax import lax
from jax.sharding import PartitionSpec as P

QUERY_HEADS = 64
KEY_VALUE_HEADS = 8
HEAD_SIZE = 128


rope_base = 1000000.0
eps_norm = 1e-06


def rotate_half(values, positions):
    half_dim = HEAD_SIZE // 2
    frequency = rope_base ** (-jnp.arange(half_dim, dtype=jnp.float32) * 2.0 / HEAD_SIZE)
    angles = positions.astype(jnp.float32)[:, None] * frequency[None, :]
    cosine = jnp.cos(angles)[:, None, :]
    sine_part = jnp.sin(angles)[:, None, :]
    lower_half = values[..., :half_dim]
    upper_half = values[..., half_dim:]
    return jnp.concatenate(
        [
            lower_half * cosine - upper_half * sine_part,
            upper_half * cosine + lower_half * sine_part,
        ],
        axis=-1,
    )


def decode_local(
    dec_queries, cache_keys, cached_value_rows, step_keys, step_values, prompt_lengths
):
    step_count, row_count, head_width = dec_queries.shape
    head_groups = QUERY_HEADS // KEY_VALUE_HEADS
    kv_local = cache_keys.shape[2] // HEAD_SIZE
    length = cache_keys.shape[1]
    score_scale = HEAD_SIZE ** (-0.5)
    query_rows = dec_queries.reshape(step_count, row_count, kv_local, head_groups, HEAD_SIZE)
    key_matrix = cache_keys.reshape(row_count, length, kv_local, HEAD_SIZE)
    value_matrix = cached_value_rows.reshape(row_count, length, kv_local, HEAD_SIZE)
    latest_key = step_keys.reshape(step_count, row_count, kv_local, HEAD_SIZE)
    latest_value = step_values.reshape(step_count, row_count, kv_local, HEAD_SIZE)
    cached = (
        jnp.einsum("srkgd,rckd->srkgc", query_rows, key_matrix, preferred_element_type=jnp.float32)
        * score_scale
    )
    live_mask = jnp.arange(length, dtype=jnp.int32)[None, :] < prompt_lengths[:, None]
    cached = jnp.where(live_mask[None, :, None, None, :], cached, -jnp.inf)
    recent = (
        jnp.einsum("srkgd,urkd->srkgu", query_rows, latest_key, preferred_element_type=jnp.float32)
        * score_scale
    )
    causal = jnp.arange(step_count)[None, :] <= jnp.arange(step_count)[:, None]
    recent = jnp.where(causal[:, None, None, None, :], recent, -jnp.inf)
    highest = jnp.maximum(jnp.max(cached, axis=-1), jnp.max(recent, axis=-1))[..., None]
    cached_w = jnp.exp(cached - highest)
    recent_w = jnp.exp(recent - highest)
    totals = jnp.sum(cached_w, axis=-1, keepdims=True) + jnp.sum(recent_w, axis=-1, keepdims=True)
    cached_w = (cached_w / totals).astype(jnp.bfloat16)
    recent_w = (recent_w / totals).astype(jnp.bfloat16)
    output = jnp.einsum(
        "srkgc,rckd->srkgd", cached_w, value_matrix, preferred_element_type=jnp.float32
    )
    output = output + jnp.einsum(
        "srkgu,urkd->srkgd", recent_w, latest_value, preferred_element_type=jnp.float32
    )
    return output.reshape(step_count, row_count, head_width).astype(jnp.bfloat16)


def attend_packed(query_raw, unscaled_pairs, doc_ids, token_row, covered):
    token_count = query_raw.shape[0]
    kv_count = unscaled_pairs.shape[2] // HEAD_SIZE
    head_groups = QUERY_HEADS // KEY_VALUE_HEADS
    query_rows = rotate_half(
        query_raw.reshape(token_count, kv_count * head_groups, HEAD_SIZE), token_row
    ).astype(jnp.bfloat16)
    key_matrix = rotate_half(
        unscaled_pairs[:, 0].reshape(token_count, kv_count, HEAD_SIZE), token_row
    ).astype(jnp.bfloat16)
    value_matrix = (
        unscaled_pairs[:, 1].reshape(token_count, kv_count, HEAD_SIZE).astype(jnp.bfloat16)
    )
    query_rows = query_rows.reshape(token_count, kv_count, head_groups, HEAD_SIZE)
    scores = jnp.einsum(
        "tkgd,skd->kgts", query_rows, key_matrix, preferred_element_type=jnp.float32
    ) * HEAD_SIZE ** (-0.5)
    indices = jnp.arange(token_count, dtype=jnp.int32)
    allowed = (doc_ids[:, None] == doc_ids[None, :]) & (indices[None, :] <= indices[:, None])
    scores = jnp.where(allowed, scores, -jnp.inf)
    highest = jnp.max(scores, axis=-1, keepdims=True)
    weights = jnp.exp(scores - highest)
    weights = (weights / jnp.sum(weights, axis=-1, keepdims=True)).astype(jnp.bfloat16)
    output = jnp.einsum("kgts,skd->tkgd", weights, value_matrix, preferred_element_type=jnp.float32)
    output = jnp.where(covered[:, None, None, None], output, 0.0)
    return output.reshape(token_count, kv_count * head_groups * HEAD_SIZE).astype(jnp.bfloat16)


def normalize(rows, norm_gain):
    wide = rows.astype(jnp.float32)
    return (
        wide
        * lax.rsqrt(jnp.mean(wide * wide, axis=1, keepdims=True) + eps_norm)
        * norm_gain[None, :]
    ).astype(jnp.bfloat16)


def on_device(
    dec_queries,
    cache_keys,
    cached_value_rows,
    step_keys,
    step_values,
    prompt_lengths,
    resp_embed,
    resp_ids,
    resp_lengths,
    dest_shard,
    dest_offset,
    norm_gain,
    w_q,
    key_value_weight,
    bias_q,
    key_value_bias,
):
    decode_out = decode_local(
        dec_queries, cache_keys, cached_value_rows, step_keys, step_values, prompt_lengths
    )
    nshard = lax.axis_size("fsdp")
    resp_count = resp_lengths.shape[0]
    resp_span = resp_embed.shape[1]
    packed_len = resp_count * resp_span
    capacity = 2 * resp_count // nshard
    indices = jnp.arange(resp_count, dtype=jnp.int32)
    earlier = (dest_shard[None, :] == dest_shard[:, None]) & (indices[None, :] < indices[:, None])
    pair_rank = jnp.sum(earlier.astype(jnp.int32), axis=1)
    placing = (dest_shard[:, None, None] == jnp.arange(nshard, dtype=jnp.int32)[None, :, None]) & (
        pair_rank[:, None, None] == jnp.arange(capacity, dtype=jnp.int32)[None, None, :]
    )
    slot_rows = jnp.einsum(
        "kpc,krx->pcrx",
        placing.astype(jnp.bfloat16),
        resp_embed,
        preferred_element_type=jnp.float32,
    ).astype(jnp.bfloat16)
    slot_ids = jnp.sum(jnp.where(placing[:, :, :, None], resp_ids[:, None, None, :], 0), axis=0)
    slot_lengths = jnp.sum(jnp.where(placing, resp_lengths[:, None, None], 0), axis=0)
    slot_offsets = jnp.sum(jnp.where(placing, dest_offset[:, None, None], 0), axis=0)
    slot_meta = jnp.stack([slot_lengths, slot_offsets], axis=-1)
    arrived, arrived_ids, arrived_meta = (
        lax.all_to_all(slot_rows, "fsdp", split_axis=0, concat_axis=0, tiled=True),
        lax.all_to_all(slot_ids, "fsdp", split_axis=0, concat_axis=0, tiled=True),
        lax.all_to_all(slot_meta, "fsdp", split_axis=0, concat_axis=0, tiled=True),
    )
    slot_total = nshard * capacity
    flat_rows = arrived.reshape(slot_total * resp_span, arrived.shape[3])
    flat_ids = arrived_ids.reshape(slot_total * resp_span)
    lengths_in = arrived_meta[:, :, 0].reshape(slot_total)
    offsets_in = arrived_meta[:, :, 1].reshape(slot_total)
    position = jnp.arange(packed_len, dtype=jnp.int32)
    inside = (position[:, None] >= offsets_in[None, :]) & (
        position[:, None] < (offsets_in + lengths_in)[None, :]
    )
    covered = jnp.any(inside, axis=1)
    slot_pick = jnp.sum(
        jnp.where(inside, jnp.arange(slot_total, dtype=jnp.int32)[None, :], 0), axis=1
    )
    token_row = jnp.where(
        covered, position - jnp.sum(jnp.where(inside, offsets_in[None, :], 0), axis=1), 0
    )
    source_row = jnp.where(covered, slot_pick * resp_span + token_row, 0)
    tokens = jnp.where(covered[:, None], flat_rows[source_row], jnp.zeros((), jnp.bfloat16))
    packed_ids = jnp.where(covered, flat_ids[source_row], -1).astype(jnp.int32)
    doc_ids = jnp.where(covered, slot_pick, -1)
    full_rows = lax.all_gather(tokens, "tp", axis=1, tiled=True)
    scaled_input = normalize(full_rows, norm_gain)
    q_width = w_q.shape[1]
    pair_width = key_value_weight.shape[1] * key_value_weight.shape[2]
    w_pairs = key_value_weight.reshape(key_value_weight.shape[0], pair_width)

    def add_rows(totals, piece_rows):
        columns = lax.slice_in_dim(scaled_input, 0, piece_rows.shape[0], axis=1)
        return totals + jnp.dot(columns, piece_rows, preferred_element_type=jnp.float32)

    empty_q = jnp.zeros((packed_len, q_width), jnp.float32)
    empty_pairs = jnp.zeros((packed_len, pair_width), jnp.float32)
    query_raw = add_rows(empty_q, lax.all_gather(w_q, "fsdp", axis=0, tiled=True))
    unscaled_pairs = add_rows(empty_pairs, lax.all_gather(w_pairs, "fsdp", axis=0, tiled=True))
    query_raw = query_raw + bias_q[None, :]
    unscaled_pairs = unscaled_pairs.reshape(packed_len, 2, pair_width // 2) + key_value_bias[None]
    ref_attn = attend_packed(query_raw, unscaled_pairs, doc_ids, token_row, covered)
    return (decode_out, packed_ids, ref_attn)


def solution(mesh):
    in_specs = (
        P(None, "fsdp", "tp"),
        P("fsdp", None, "tp"),
        P("fsdp", None, "tp"),
        P(None, "fsdp", "tp"),
        P(None, "fsdp", "tp"),
        P("fsdp"),
        P("fsdp", None, "tp"),
        P("fsdp", None),
        P("fsdp"),
        P("fsdp"),
        P("fsdp"),
        P(),
        P("fsdp", "tp"),
        P("fsdp", None, "tp"),
        P("tp"),
        P(None, "tp"),
    )
    out_specs = (P(None, "fsdp", "tp"), P("fsdp"), P("fsdp", "tp"))
    return jax.shard_map(
        on_device, mesh=mesh, in_specs=in_specs, out_specs=out_specs, check_vma=False
    )
```

profile of v0, /device:TPU:0, one launch (start us, length us, event | category | flops | bytes accessed | tf_op | source)
XLA Modules:
  0.0 522.4 jit_solution(5296255659046227444)
XLA Ops:
  7.2 0.9 convert_reduce_fusion
  8.1 0.7 iota_compare_fusion.5
  8.7 0.9 select_reduce_fusion.4
  9.7 0.7 copy.110
  10.3 5.2 all-to-all-start
  15.5 4.2 convolution_convert_fusion
  19.7 4.3 copy.114
  24.0 4.5 all-to-all-start.2
  28.5 0.0 all-gather.4.cloned.1.call-start
  28.6 0.1 ge.18
  28.7 0.1 reshape_squeeze.8
  28.8 0.1 fusion.41
  28.9 0.1 select_reduce_fusion.1
  29.0 48.6 %all-to-all-done.2 = bf16[8,4,32,2048]{3,2,1,0:T(8,128)(2,1)} async-done(((bf16[8,4,32,2048]{3,2,1,0:T(8,128)(2,1)}), bf16[8,4,32,2048]{3,2,1,0:T(8,128)(2,1)}, u32[]{:S(2)}, u32[]{:S(2)}) %all-to-all-start.2) | async-done | bytes 4194336 | tf_op jit(solution)/shard_map/all_to_all | solution.py:152
  77.7 7.1 %gather_fusion.1 = bf16[512,2048]{1,0:T(8,128)(2,1)S(1)} fusion(bf16[1024,2048]{1,0:T(8,128)(2,1)} %bitcast.15, s32[1024]{0:T(1024)S(1)} %pad_clamp_fusion), kind=kCustom, calls=%fused_computation.1 | custom fusion | bytes 4196352 | tf_op jit(solution)/shard_map/gather | solution.py:173
  84.8 0.0 copy-start.1
  84.8 1.5 broadcast_select_fusion
  86.3 0.0 all-gather.4.cloned.1.call-update
  86.4 0.0 copy-start.2
  86.4 0.0 copy-start.5
  86.4 0.0 all-gather.6.cloned.1.call-start
  86.5 1.2 copy.139
  87.7 0.0 all-gather.6.cloned.1.call-update
  87.7 0.0 all-gather.8.cloned.1.call-start
  87.8 0.7 all-gather.8.cloned.1.call-update
  88.5 0.1 copy.111
  88.6 0.1 select_reduce_fusion
  88.7 0.7 reshape.321
  89.4 3.5 all-to-all-start.1
  93.0 7.2 %reshape.275 = bf16[2,4096,2,128]{3,2,1,0:T(2,128)(2,1)} reshape(bf16[2,4096,256]{2,1,0:T(8,128)(2,1)} %param.17) | data formatting | bytes 8388608 | tf_op jit(solution)/shard_map/reshape | solution.py:41
  100.2 6.9 %reshape.278 = bf16[2,4096,2,128]{3,2,1,0:T(2,128)(2,1)} reshape(bf16[2,4096,256]{2,1,0:T(8,128)(2,1)} %param.18) | data formatting | bytes 8388608 | tf_op jit(solution)/shard_map/reshape | solution.py:42
  107.2 0.2 fusion.61
  107.4 0.1 iota_compare_fusion.3
  107.5 3.6 fusion.60
  111.2 0.3 fusion.35
  111.5 0.2 fusion.50
  111.7 0.7 fusion.29
  112.4 0.6 convert_element_type.59
  113.1 1.0 multiply_cosine_fusion
  114.1 0.2 fusion.34
  114.3 0.5 broadcast.202
  114.8 0.7 reduce.8
  115.5 0.1 reshape.322
  115.5 0.1 reshape.280
  115.6 2.3 gather_fusion
  117.9 0.6 broadcast_select_fusion.2
  118.5 117.1 %all-gather.4.cloned.1.call-done = bf16[512,8192]{1,0:T(8,128)(2,1)} async-done(((bf16[512,2048]{1,0:T(8,128)(2,1)}), bf16[512,8192]{1,0:T(8,128)(2,1)}) %all-gather.4.cloned.1.call-update) | async-done | bytes 8388624 | tf_op jit(solution)/shard_map/all_gather | solution.py:176
  235.6 5.1 fusion.1
  240.7 49.4 %all-gather.6.cloned.1.call-done = bf16[8192,512]{1,0:T(8,128)(2,1)} async-done(((bf16[1024,512]{1,0:T(8,128)(2,1)}), bf16[8192,512]{1,0:T(8,128)(2,1)}) %all-gather.6.cloned.1.call-update) | async-done | bytes 8388624 | tf_op jit(solution)/shard_map/all_gather | solution.py:189
  290.1 11.4 %fusion.15 = f32[512,512]{0,1:T(8,128)S(1)} fusion(bf16[8192,512]{1,0:T(8,128)(2,1)} %all-gather.6.cloned.1.call-done, bf16[512,8192]{1,0:T(8,128)(2,1)} %all-gather.4.cloned.1.call-done, f32[8192]{0:T(1024)S(1)} %copy-done.8, f32[512]{0:T(512)S(1)} %add_rsqrt_fusion), kind=kOutput, calls=%fused_computation.27 | convolution fusion | flops 4311744512 | bytes 17860608 | tf_op jit(solution)/shard_map/dot_general | solution.py:184
  301.5 0.1 broadcast_add_fusion
  301.7 0.2 copy.138
  301.9 0.2 copy.137
  302.2 0.1 subtract_convert_fusion.1
  302.3 150.5 %all-gather.8.cloned.1.call-done = bf16[8192,2048]{1,0:T(8,128)(2,1)} async-done(((bf16[1024,2048]{1,0:T(8,128)(2,1)}), bf16[8192,2048]{1,0:T(8,128)(2,1)}) %all-gather.8.cloned.1.call-update) | async-done | bytes 33554448 | tf_op jit(solution)/shard_map/all_gather | solution.py:188
  452.8 24.0 %add_bitcast_fusion = f32[64,8,16,128]{3,1,2,0:T(8,128)S(1)} fusion(bf16[8192,2048]{1,0:T(8,128)(2,1)} %all-gather.8.cloned.1.call-done, bf16[512,8192]{1,0:T(8,128)(2,1)} %all-gather.4.cloned.1.call-done, f32[8192]{0:T(1024)S(1)} %copy-done.8, f32[512]{0:T(512)S(1)} %add_rsqrt_fusion, f32[2048]{0:T(1024)S(1)} %copy-done.9), kind=kOutput, calls=%fused_computation.25 | convolution fusion | flops 17197694976 | bytes 46180352 | tf_op jit(solution)/shard_map/dot_general | solution.py:184
  476.8 0.9 copy.140
  477.8 1.8 subtract_convert_fusion
  479.6 0.5 copy.118
  480.1 0.5 copy.117
  480.7 8.2 %fusion.17 = f32[2,512,512,8]{2,1,3,0:T(8,128)} fusion(bf16[512,2,8,64]{3,0,2,1:T(8,128)(2,1)S(1)} %bitcast.65, bf16[512,2,8,64]{3,0,2,1:T(8,128)(2,1)S(1)} %bitcast.66, bf16[512,2,64]{2,0,1:T(8,128)(2,1)S(1)} %get-tuple-element.30, bf16[512,2,64]{2,0,1:T(8,128)(2,1)S(1)} %get-tuple-element.29), kind=kOutput, calls=%fused_computation.28 | convolution fusion | flops 1078460416 | bytes 19136512 | tf_op jit(solution)/shard_map/tkgd,skd->kgts/dot_general | solution.py:86
  488.8 17.3 %fusion.62 = (f32[2,8,512]{2,1,0:T(8,128)S(1)}, f32[2,8,512,512]{2,3,1,0:T(8,128)}) fusion(f32[2,512,512,8]{2,1,3,0:T(8,128)} %fusion.17, pred[512,512]{0,1:T(8,128)(4,1)S(1)} %fusion.34), kind=kOutput, calls=%fused_computation.108 | output fusion | flops 25166336 | bytes 33849344 | tf_op jit(solution)/shard_map/sub | solution.py:93
  506.1 7.4 %select_convert_fusion = bf16[2,128,8,512]{3,1,2,0:T(8,128)(2,1)S(1)} fusion(pred[512]{0:T(512)(128)(4,1)S(1)} %fusion.41, bf16[512,2,128,1]{0,2,3,1:T(8,128)(2,1)S(1)} %bitcast.74, f32[2,8,512,512]{2,3,1,0:T(8,128)} %get-tuple-element.43, f32[2,8,512]{2,1,0:T(8,128)S(1)} %get-tuple-element.42), kind=kOutput, calls=%fused_computation.22 | convolution fusion | flops 1084227584 | bytes 19169792 | tf_op jit(solution)/shard_map/kgts,skd->tkgd/dot_general | solution.py:95
  513.5 2.4 copy.120
  (41 shorter events, 0.4 us)
Async XLA Ops:
  10.3 13.6 %all-to-all-start = ((s32[8,4,2]{1,2,0:T(2,128)}), s32[8,4,2]{1,2,0:T(2,128)S(1)}, u32[]{:S(2)}, u32[]{:S(2)}) async-start(s32[8,4,2]{1,2,0:T(2,128)} %copy.110), calls=%async_computation | async-start | bytes 16384 | tf_op jit(solution)/shard_map/all_to_all | solution.py:154
  24.0 53.7 %all-to-all-start.2 = ((bf16[8,4,32,2048]{3,2,1,0:T(8,128)(2,1)}), bf16[8,4,32,2048]{3,2,1,0:T(8,128)(2,1)}, u32[]{:S(2)}, u32[]{:S(2)}) async-start(bf16[8,4,32,2048]{3,2,1,0:T(8,128)(2,1)} %copy.114), calls=%async_computation.2 | async-start | bytes 8388608 | tf_op jit(solution)/shard_map/all_to_all | solution.py:152
  28.5 207.0 %all-gather.4.cloned.1.call-start = ((), (), s32[]{:S(2)}) async-start(), calls=%async_computation.3 | async-start | bytes 10485760 | tf_op jit(solution)/shard_map/all_gather | solution.py:176
  84.8 1.7 copy-start.1
  86.4 2.2 copy-start.3
  86.4 6.5 %copy-start.2 = (bf16[2,2,2048]{2,1,0:T(2,128)(2,1)S(1)}, bf16[2,2,2048]{2,1,0:T(2,128)(2,1)}, u32[]{:S(2)}) copy-start(bf16[2,2,2048]{2,1,0:T(2,128)(2,1)} %param.16) | copy-start | bytes 49156
  86.4 6.6 %copy-start.5 = (bf16[2,2,256]{2,1,0:T(2,128)(2,1)S(1)}, bf16[2,2,256]{2,1,0:T(2,128)(2,1)}, u32[]{:S(2)}) copy-start(bf16[2,2,256]{2,1,0:T(2,128)(2,1)} %param.19) | copy-start | bytes 6148
  86.4 203.7 %all-gather.6.cloned.1.call-start = ((), (), s32[]{:S(2)}) async-start(), calls=%async_computation.4 | async-start | bytes 9437184 | tf_op jit(solution)/shard_map/all_gather | solution.py:189
  87.7 365.1 %all-gather.8.cloned.1.call-start = ((), (), s32[]{:S(2)}) async-start(), calls=%async_computation.5 | async-start | bytes 37748736 | tf_op jit(solution)/shard_map/all_gather | solution.py:188
  89.4 24.9 %all-to-all-start.1 = ((s32[8,1,128]{2,1,0:T(1,128)}), s32[8,1,128]{2,1,0:T(1,128)S(1)}, u32[]{:S(2)}, u32[]{:S(2)}) async-start(s32[8,1,128]{2,1,0:T(1,128)} %reshape.321), calls=%async_computation.1 | async-start | bytes 8192 | tf_op jit(solution)/shard_map/all_to_all | solution.py:153
  93.0 7.2 %copy-start.6 = (bf16[2,2,256]{2,1,0:T(2,128)(2,1)S(1)}, bf16[2,2,256]{2,1,0:T(2,128)(2,1)}, u32[]{:S(2)}) copy-start(bf16[2,2,256]{2,1,0:T(2,128)(2,1)} %param.20) | copy-start | bytes 6148
  100.2 7.2 %copy-start.7 = (s32[2]{0:T(128)S(1)}, s32[2]{0:T(128)}, u32[]{:S(2)}) copy-start(s32[2]{0:T(128)} %param.21) | copy-start | bytes 28
  107.2 4.5 copy-start
  118.5 171.6 %copy-start.8 = (f32[8192]{0:T(1024)S(1)}, f32[8192]{0:T(1024)}, u32[]{:S(2)}) copy-start(f32[8192]{0:T(1024)} %param.27) | copy-start | bytes 98308
  240.7 60.8 %copy-start.4 = (f32[2,256]{1,0:T(2,128)S(1)}, f32[2,256]{1,0:T(2,128)}, u32[]{:S(2)}) copy-start(f32[2,256]{1,0:T(2,128)} %param.31) | copy-start | bytes 6148
  301.5 151.3 %copy-start.9 = (f32[2048]{0:T(1024)S(1)}, f32[2048]{0:T(1024)}, u32[]{:S(2)}) copy-start(f32[2048]{0:T(1024)} %param.30) | copy-start | bytes 24580
Sparse Core Ops, SparseCore 0:
  86.5 149.0 all-gather.3
  237.5 52.5 all-gather.5
  292.0 160.7 all-gather.7
where the time goes:
time: 523 us; the launch traced here: 522 us
  waiting for transfers between devices  366 us (70%)
  matrix products  59.9 us (11%)
  local copies, waits for them, and re-layouts  37 us (7%)
  other arithmetic  31.8 us (6%)
  between operations  14.1 us (3%)
  starting transfers between devices  13.4 us (3%)
    all_gather x1, waiting for transfers between devices, on_device(): lax.all_gather(w_q, 'fsdp', axis=0, tiled=True)  150 us
    all_gather x1, waiting for transfers between devices, on_device(): full_rows = lax.all_gather(tokens, 'tp', axis=1, tiled=True)  117 us
    all_gather x1, waiting for transfers between devices, on_device(): lax.all_gather(w_pairs, 'fsdp', axis=0, tiled=True)  49.4 us
    all_to_all x1, waiting for transfers between devices, on_device(): lax.all_to_all(slot_rows, 'fsdp', split_axis=0, concat_axis=0, tiled=True)  48.6 us
    dot_general x2, matrix products, add_rows(): jnp.dot(columns, piece_rows, preferred_element_type=jnp.float32)  35.4 us
    sub x1, other arithmetic, attend_packed(): weights = jnp.exp(scores - highest)  17.3 us
  transfers between devices with their start and end apart: 6, of which 4 were waited for; matrix products, arithmetic and copies ran while one was open for 10% of the time, Pallas kernels for 0%

commit v1 on v0

v1 whole, which is shorter than its diff:
```python
import jax
import jax.numpy as jnp
from jax import lax
from jax.sharding import PartitionSpec as P

QUERY_HEADS = 64
KEY_VALUE_HEADS = 8
HEAD_SIZE = 128


rope_base = 1000000.0
eps_norm = 1e-06


def rotary_table(span):
    half_dim = HEAD_SIZE // 2
    frequency = rope_base ** (-jnp.arange(half_dim, dtype=jnp.float32) * 2.0 / HEAD_SIZE)
    angles = jnp.arange(span, dtype=jnp.int32).astype(jnp.float32)[:, None] * frequency[None, :]
    return jnp.cos(angles)[None, :, None, :], jnp.sin(angles)[None, :, None, :]


def rotate_half(values, table):
    cosine, sine_part = table
    half_dim = HEAD_SIZE // 2
    lower_half = values[..., :half_dim]
    upper_half = values[..., half_dim:]
    return jnp.concatenate(
        [
            lower_half * cosine - upper_half * sine_part,
            upper_half * cosine + lower_half * sine_part,
        ],
        axis=-1,
    )


def decode_local(
    dec_queries, cache_keys, cached_value_rows, step_keys, step_values, prompt_lengths
):
    step_count, row_count, head_width = dec_queries.shape
    head_groups = QUERY_HEADS // KEY_VALUE_HEADS
    kv_local = cache_keys.shape[2] // HEAD_SIZE
    length = cache_keys.shape[1]
    score_scale = HEAD_SIZE ** (-0.5)
    query_rows = dec_queries.reshape(step_count, row_count, kv_local, head_groups, HEAD_SIZE)
    key_matrix = cache_keys.reshape(row_count, length, kv_local, HEAD_SIZE)
    value_matrix = cached_value_rows.reshape(row_count, length, kv_local, HEAD_SIZE)
    latest_key = step_keys.reshape(step_count, row_count, kv_local, HEAD_SIZE)
    latest_value = step_values.reshape(step_count, row_count, kv_local, HEAD_SIZE)
    cached = (
        jnp.einsum("srkgd,rckd->srkgc", query_rows, key_matrix, preferred_element_type=jnp.float32)
        * score_scale
    )
    live_mask = jnp.arange(length, dtype=jnp.int32)[None, :] < prompt_lengths[:, None]
    cached = jnp.where(live_mask[None, :, None, None, :], cached, -jnp.inf)
    recent = (
        jnp.einsum("srkgd,urkd->srkgu", query_rows, latest_key, preferred_element_type=jnp.float32)
        * score_scale
    )
    causal = jnp.arange(step_count)[None, :] <= jnp.arange(step_count)[:, None]
    recent = jnp.where(causal[:, None, None, None, :], recent, -jnp.inf)
    highest = jnp.maximum(jnp.max(cached, axis=-1), jnp.max(recent, axis=-1))[..., None]
    cached_w = jnp.exp(cached - highest)
    recent_w = jnp.exp(recent - highest)
    totals = jnp.sum(cached_w, axis=-1, keepdims=True) + jnp.sum(recent_w, axis=-1, keepdims=True)
    cached_w = (cached_w / totals).astype(jnp.bfloat16)
    recent_w = (recent_w / totals).astype(jnp.bfloat16)
    output = jnp.einsum(
        "srkgc,rckd->srkgd", cached_w, value_matrix, preferred_element_type=jnp.float32
    )
    output = output + jnp.einsum(
        "srkgu,urkd->srkgd", recent_w, latest_value, preferred_element_type=jnp.float32
    )
    return output.reshape(step_count, row_count, head_width).astype(jnp.bfloat16)


def attend_responses(query_raw, key_rows, value_rows, table):
    resp_count, span, kv_width = key_rows.shape
    heads = query_raw.shape[1] // HEAD_SIZE
    query_rows = rotate_half(query_raw.reshape(resp_count, span, heads, HEAD_SIZE), table).astype(
        jnp.bfloat16
    )
    scores = jnp.einsum(
        "btgd,bsd->bgts", query_rows, key_rows, preferred_element_type=jnp.float32
    ) * HEAD_SIZE ** (-0.5)
    indices = jnp.arange(span, dtype=jnp.int32)
    scores = jnp.where(indices[None, :] <= indices[:, None], scores, -jnp.inf)
    highest = jnp.max(scores, axis=-1, keepdims=True)
    weights = jnp.exp(scores - highest)
    weights = (weights / jnp.sum(weights, axis=-1, keepdims=True)).astype(jnp.bfloat16)
    output = jnp.einsum("bgts,bsd->btgd", weights, value_rows, preferred_element_type=jnp.float32)
    return output.reshape(resp_count, span, heads * HEAD_SIZE).astype(jnp.bfloat16)


def normalize(blocks, norm_gain):
    wide = blocks.astype(jnp.float32)
    count = blocks.shape[0] * blocks.shape[2]
    mean = jnp.sum(wide * wide, axis=(0, 2), keepdims=True) / count
    gain = norm_gain.reshape(blocks.shape[0], 1, blocks.shape[2])
    return (wide * lax.rsqrt(mean + eps_norm) * gain).astype(jnp.bfloat16)


def swap(value, nshard, bit):
    return lax.ppermute(value, "fsdp", [(i, i ^ bit) for i in range(nshard)])


def gather_rows(piece, sibling_piece, nshard):
    depth = piece.shape[0]
    half = depth // 2
    over_x = swap(piece, nshard, 2)
    over_y = swap(piece, nshard, 4)
    far_low = swap(over_x[:half], nshard, 4)
    far_high = swap(over_y[half:], nshard, 2)
    return [
        (0, 0, piece),
        (1, 0, sibling_piece),
        (2, 0, over_x),
        (3, 0, swap(over_x, nshard, 1)),
        (4, 0, over_y),
        (5, 0, swap(over_y, nshard, 1)),
        (6, 0, far_low),
        (7, 0, swap(far_low, nshard, 1)),
        (6, half, far_high),
        (7, half, swap(far_high, nshard, 1)),
    ]


def on_device(
    dec_queries,
    cache_keys,
    cached_value_rows,
    step_keys,
    step_values,
    prompt_lengths,
    resp_embed,
    resp_ids,
    resp_lengths,
    dest_shard,
    dest_offset,
    norm_gain,
    w_q,
    key_value_weight,
    bias_q,
    key_value_bias,
):
    nshard = lax.axis_size("fsdp")
    me = lax.axis_index("fsdp")
    resp_count, resp_span, feature_width = resp_embed.shape
    packed_len = resp_count * resp_span
    full_rows = lax.all_gather(
        resp_embed.reshape(packed_len, feature_width), "tp", axis=0, tiled=False
    )
    pair_width = key_value_weight.shape[1] * key_value_weight.shape[2]
    kv_width = pair_width // 2
    kv_count = kv_width // HEAD_SIZE
    w_pairs = key_value_weight.reshape(key_value_weight.shape[0], pair_width)
    q_width = w_q.shape[1]
    chunk = (QUERY_HEADS // KEY_VALUE_HEADS) * HEAD_SIZE // 2
    pieces = [w_pairs] + [w_q[:, i : i + chunk] for i in range(0, q_width, chunk)]
    if nshard == 8:
        sibling_q = swap(w_q, nshard, 1)
        sibling_pieces = [swap(w_pairs, nshard, 1)] + [
            sibling_q[:, i : i + chunk] for i in range(0, q_width, chunk)
        ]
        gathered = [gather_rows(p, s, nshard) for p, s in zip(pieces, sibling_pieces)]
    else:
        gathered = [[(0, 0, lax.all_gather(p, "fsdp", axis=0, tiled=True))] for p in pieces]

    decode_out = decode_local(
        dec_queries, cache_keys, cached_value_rows, step_keys, step_values, prompt_lengths
    )

    capacity = 2 * resp_count // nshard
    indices = jnp.arange(resp_count, dtype=jnp.int32)
    earlier = (dest_shard[None, :] == dest_shard[:, None]) & (indices[None, :] < indices[:, None])
    pair_rank = jnp.sum(earlier.astype(jnp.int32), axis=1)
    placing = (dest_shard[:, None, None] == jnp.arange(nshard, dtype=jnp.int32)[None, :, None]) & (
        pair_rank[:, None, None] == jnp.arange(capacity, dtype=jnp.int32)[None, None, :]
    )
    facts = jnp.concatenate([resp_ids, resp_lengths[:, None], dest_offset[:, None]], axis=1)
    slot_facts = jnp.sum(jnp.where(placing[:, :, :, None], facts[:, None, None, :], 0), axis=0)
    arrived_facts = lax.all_to_all(slot_facts, "fsdp", split_axis=0, concat_axis=0, tiled=True)
    slot_total = nshard * capacity
    arrived_facts = arrived_facts.reshape(slot_total, resp_span + 2)
    ids_in = arrived_facts[:, :resp_span]
    lengths_in = arrived_facts[:, resp_span]
    offsets_in = arrived_facts[:, resp_span + 1]
    position = jnp.arange(packed_len, dtype=jnp.int32)
    picks = (
        position[:, None, None]
        == offsets_in[None, :, None] + jnp.arange(resp_span, dtype=jnp.int32)[None, None, :]
    ) & (jnp.arange(resp_span, dtype=jnp.int32)[None, None, :] < lengths_in[None, :, None])
    picks = picks.reshape(packed_len, slot_total * resp_span)
    packed_ids = jnp.sum(
        jnp.where(picks, ids_in.reshape(1, slot_total * resp_span) + 1, 0), axis=1
    ) - 1
    picks = picks.astype(jnp.bfloat16)

    normed = normalize(full_rows, norm_gain)
    block_rows = w_q.shape[0]
    if nshard == 8:
        per_block = feature_width // block_rows
        sources = []
        for bits in range(nshard):
            owner = jnp.bitwise_xor(me, bits)
            sources.append(
                lax.dynamic_slice(
                    normed,
                    (owner // per_block, 0, (owner % per_block) * block_rows),
                    (1, packed_len, block_rows),
                )[0]
            )
    else:
        sources = [jnp.swapaxes(normed, 0, 1).reshape(packed_len, -1)]

    def project(blocks):
        total = None
        for bits, first, rows in blocks:
            columns = lax.slice_in_dim(sources[bits], first, first + rows.shape[0], axis=1)
            part = jnp.dot(columns, rows, preferred_element_type=jnp.float32)
            total = part if total is None else total + part
        return total

    table = rotary_table(resp_span)
    pair_raw = project(gathered[0]).reshape(packed_len, 2, kv_width) + key_value_bias[None]
    ref_keys = rotate_half(
        pair_raw[:, 0].reshape(resp_count, resp_span, kv_count, HEAD_SIZE), table
    ).astype(jnp.bfloat16)
    ref_values = (
        pair_raw[:, 1].reshape(resp_count, resp_span, kv_count, HEAD_SIZE).astype(jnp.bfloat16)
    )
    spread = jnp.swapaxes(placing.reshape(resp_count, slot_total), 0, 1).astype(jnp.bfloat16)
    results = []
    for i, blocks in enumerate(gathered[1:]):
        query_raw = project(blocks) + bias_q[None, i * chunk : (i + 1) * chunk]
        kv_head = i // 2
        attn = attend_responses(query_raw, ref_keys[:, :, kv_head], ref_values[:, :, kv_head], table)
        slots = jnp.einsum(
            "sk,krx->srx", spread, attn, preferred_element_type=jnp.float32
        ).astype(jnp.bfloat16)
        slots = slots.reshape(nshard, capacity * resp_span, chunk)
        arrived = lax.all_to_all(slots, "fsdp", split_axis=0, concat_axis=0, tiled=True)
        arrived = arrived.reshape(slot_total * resp_span, chunk)
        results.append(
            jnp.dot(picks, arrived, preferred_element_type=jnp.float32).astype(jnp.bfloat16)
        )
    ref_attn = jnp.concatenate(results, axis=1)
    return (decode_out, packed_ids, ref_attn)


def solution(mesh):
    in_specs = (
        P(None, "fsdp", "tp"),
        P("fsdp", None, "tp"),
        P("fsdp", None, "tp"),
        P(None, "fsdp", "tp"),
        P(None, "fsdp", "tp"),
        P("fsdp"),
        P("fsdp", None, "tp"),
        P("fsdp", None),
        P("fsdp"),
        P("fsdp"),
        P("fsdp"),
        P(),
        P("fsdp", "tp"),
        P("fsdp", None, "tp"),
        P("tp"),
        P(None, "tp"),
    )
    out_specs = (P(None, "fsdp", "tp"), P("fsdp"), P("fsdp", "tp"))
    return jax.shard_map(
        on_device, mesh=mesh, in_specs=in_specs, out_specs=out_specs, check_vma=False
    )
```

time: 523 us -> 413 us (0.79); the launches traced: 522 us -> 407 us
  waiting for transfers between devices: 366 us -> 134 us
  matrix products: 59.9 us -> 108 us
  starting transfers between devices: 13.4 us -> 54.1 us
  local copies, waits for them, and re-layouts: 37 us -> 71.8 us
  other arithmetic: 31.8 us -> 23.4 us
    all_gather x3 -> x1, waiting for transfers between devices: 317 us -> 27.1 us  [on_device(): lax.all_gather(resp_embed.reshape(packed_len, feature_width), 'tp', axis=...]
    ppermute x0 -> x42, waiting for transfers between devices: none -> 77.9 us  [swap(): return lax.ppermute(value, 'fsdp', [(i, i ^ bit) for i in range(nshard)])]
    dot_general x5 -> x62, matrix products: 55.1 us -> 92.8 us  [the longest x50 76.5 us: project(): part = jnp.dot(columns, rows, preferred_element_type=jnp.float32)]
    ppermute x0 -> x42, starting transfers between devices: none -> 35.6 us  [swap(): return lax.ppermute(value, 'fsdp', [(i, i ^ bit) for i in range(nshard)])]
    slice x4 -> x19, local copies, waits for them, and re-layouts: 0.13 us -> 30.3 us  [the longest x5 9.43 us: gather_rows(): far_high = swap(over_y[half:], nshard, 2)]
    all_to_all x3 -> x5, waiting for transfers between devices: 48.6 us -> 28 us  [the longest x4 28 us: on_device(): lax.all_to_all(slots, 'fsdp', split_axis=0, concat_axis=0, tiled=True)]
    sub x1, other arithmetic: 17.3 us -> 0.58 us  [on_device(): jnp.sum(jnp.where(picks, ids_in.reshape(1, slot_total * resp_span) + 1, 0...]
    convert_element_type x0 -> x2, other arithmetic: none -> 10.3 us  [the longest x1 10.3 us: normalize(): return (wide * lax.rsqrt(mean + eps_norm) * gain).astype(jnp.bfloat16)]
  transfers between devices with their start and end apart: 6 -> 48, of which waited for: 4 -> 19; matrix products, arithmetic and copies ran while one was open for 10% -> 49% of each run, Pallas kernels for 0% -> 0%
where the time goes in v1:
time: 413 us; the launch traced here: 407 us
  waiting for transfers between devices  134 us (32%)
  matrix products  108 us (26%)
  local copies, waits for them, and re-layouts  71.8 us (17%)
  starting transfers between devices  54.1 us (13%)
  other arithmetic  23.4 us (6%)
  between operations  16.2 us (4%)
    ppermute x42, waiting for transfers between devices, swap(): return lax.ppermute(value, 'fsdp', [(i, i ^ bit) for i in range(nshard)])  77.9 us
    dot_general x50, matrix products, project(): part = jnp.dot(columns, rows, preferred_element_type=jnp.float32)  76.5 us
    ppermute x42, starting transfers between devices, swap(): return lax.ppermute(value, 'fsdp', [(i, i ^ bit) for i in range(nshard)])  35.6 us
    all_to_all x4, waiting for transfers between devices, on_device(): lax.all_to_all(slots, 'fsdp', split_axis=0, concat_axis=0, tiled=True)  28 us
    all_gather x1, waiting for transfers between devices, on_device(): lax.all_gather(resp_embed.reshape(packed_len, feature_width), 'tp', axis=...  27.1 us
    all_to_all x4, starting transfers between devices, on_device(): lax.all_to_all(slots, 'fsdp', split_axis=0, concat_axis=0, tiled=True)  15.2 us
    convert_element_type x1, other arithmetic, normalize(): return (wide * lax.rsqrt(mean + eps_norm) * gain).astype(jnp.bfloat16)  10.3 us
    slice x5, local copies, waits for them, and re-layouts, gather_rows(): far_high = swap(over_y[half:], nshard, 2)  9.43 us
  transfers between devices with their start and end apart: 48, of which 19 were waited for; matrix products, arithmetic and copies ran while one was open for 49% of the time, Pallas kernels for 0%

profile of v1, /device:TPU:0, one launch (start us, length us, event | category | flops | bytes accessed | tf_op | source)
XLA Modules:
  0.0 406.7 jit_solution(11206342545690013564)
XLA Ops:
  8.0 4.3 %fusion.340 = (bf16[1024,512]{1,0:T(8,128)(2,1)}, bf16[1024,512]{1,0:T(8,128)(2,1)}, bf16[1024,512]{1,0:T(8,128)(2,1)}, bf16[1024,512]{1,0:T(8,128)(2,1)}) fusion(bf16[1024,2048]{1,0:T(8,128)(2,1)} %param.28), kind=kLoop, calls=%fused_computation.367 | loop fusion | bytes 8388608 | tf_op jit(solution)/shard_map/slice | solution.py:158
  12.3 2.9 collective-permute-start.34
  17.3 2.0 collective-permute-start.18
  20.7 3.3 all-to-all-start
  24.0 15.5 %collective-permute-done.34 = bf16[1024,512]{1,0:T(8,128)(2,1)} collective-permute-done((bf16[1024,512]{1,0:T(8,128)(2,1)}, bf16[1024,512]{1,0:T(8,128)(2,1)}, u32[]{:S(2)}, u32[]{:S(2)}) %collective-permute-start.34) | collective-permute-done | bytes 1048608 | tf_op jit(solution)/shard_map/ppermute | solution.py:103
  39.5 2.1 collective-permute-start.20
  43.1 7.0 %reshape.343 = bf16[2,4096,2,128]{3,2,1,0:T(2,128)(2,1)} reshape(bf16[2,4096,256]{2,1,0:T(8,128)(2,1)} %param.17) | data formatting | bytes 8388608 | tf_op jit(solution)/shard_map/reshape | solution.py:45
  50.2 3.5 fusion.348
  54.1 7.8 %collective-permute-done.26 = bf16[1024,512]{1,0:T(8,128)(2,1)S(1)} collective-permute-done((bf16[1024,512]{1,0:T(8,128)(2,1)}, bf16[1024,512]{1,0:T(8,128)(2,1)S(1)}, u32[]{:S(2)}, u32[]{:S(2)}) %collective-permute-start.26) | collective-permute-done | bytes 1048608 | tf_op jit(solution)/shard_map/ppermute | solution.py:103
  61.9 2.1 collective-permute-start.10
  65.6 18.7 %collective-permute-done.18 = bf16[1024,512]{1,0:T(8,128)(2,1)S(1)} collective-permute-done((bf16[1024,512]{1,0:T(8,128)(2,1)}, bf16[1024,512]{1,0:T(8,128)(2,1)S(1)}, u32[]{:S(2)}, u32[]{:S(2)}) %collective-permute-start.18) | collective-permute-done | bytes 1048608 | tf_op jit(solution)/shard_map/ppermute | solution.py:103
  84.4 2.1 collective-permute-start.1
  88.6 7.1 %reshape.346 = bf16[2,4096,2,128]{3,2,1,0:T(2,128)(2,1)} reshape(bf16[2,4096,256]{2,1,0:T(8,128)(2,1)} %param.18) | data formatting | bytes 8388608 | tf_op jit(solution)/shard_map/reshape | solution.py:46
  112.9 15.7 %collective-permute-done.1 = bf16[1024,512]{1,0:T(8,128)(2,1)S(1)} collective-permute-done((bf16[1024,512]{1,0:T(8,128)(2,1)}, bf16[1024,512]{1,0:T(8,128)(2,1)S(1)}, u32[]{:S(2)}, u32[]{:S(2)}) %collective-permute-start.1) | collective-permute-done | bytes 1048608 | tf_op jit(solution)/shard_map/ppermute | solution.py:103
  135.0 27.1 %all-gather.2.cloned.1.call-done = bf16[4,512,2048]{2,1,0:T(8,128)(2,1)} async-done(((bf16[1,512,2048]{2,1,0:T(8,128)(2,1)}), bf16[4,512,2048]{2,1,0:T(8,128)(2,1)}) %all-gather.2.cloned.1.call-update) | async-done | bytes 8388624 | tf_op jit(solution)/shard_map/all_gather | solution.py:149
  162.1 5.1 %fusion.4 = f32[512]{0:T(512)S(1)} fusion(bf16[4,512,2048]{2,1,0:T(8,128)(2,1)} %all-gather.2.cloned.1.call-done), kind=kLoop, calls=%fused_computation.6 | loop fusion | flops 12582400 | bytes 8390656 | tf_op jit(solution)/shard_map/reduce_sum | solution.py:97
  167.2 10.3 %fusion.6 = bf16[4,512,2048]{2,1,0:T(8,128)(2,1)} fusion(bf16[4,512,2048]{2,1,0:T(8,128)(2,1)} %all-gather.2.cloned.1.call-done, f32[4,2048]{1,0:T(4,128)S(1)} %mul.390, f32[512]{0:T(512)S(1)} %add_rsqrt_fusion), kind=kLoop, calls=%fused_computation.8 | loop fusion | flops 16777216 | bytes 16812032 | tf_op jit(solution)/shard_map/convert_element_type | solution.py:99
  177.5 2.1 fusion.117
  179.6 2.8 fusion.125
  182.5 2.2 convolution_add_fusion.5
  185.3 2.0 convolution_add_fusion.29
  187.3 3.0 convolution_add_fusion.4
  191.1 2.0 fusion.100
  199.8 8.2 %collective-permute-done.7 = bf16[512,512]{1,0:T(8,128)(2,1)S(1)} collective-permute-done((bf16[512,512]{1,0:T(8,128)(2,1)S(1)}, bf16[512,512]{1,0:T(8,128)(2,1)S(1)}, u32[]{:S(2)}, u32[]{:S(2)}) %collective-permute-start.7) | collective-permute-done | bytes 524320 | tf_op jit(solution)/shard_map/ppermute | solution.py:103
  209.3 1.9 convolution_add_fusion.11
  214.4 3.0 fusion.92
  217.3 2.6 copy.222
  219.9 2.4 convolution_add_fusion.10
  226.8 2.9 fusion.34
  230.3 2.3 fusion.33
  236.4 1.9 convolution_add_fusion.17
  239.1 1.9 fusion.94
  247.6 1.9 fusion.96
  258.6 5.6 %collective-permute-done.14 = bf16[512,512]{1,0:T(8,128)(2,1)} collective-permute-done((bf16[512,512]{1,0:T(8,128)(2,1)S(1)}, bf16[512,512]{1,0:T(8,128)(2,1)}, u32[]{:S(2)}, u32[]{:S(2)}) %collective-permute-start.14) | collective-permute-done | bytes 524320 | tf_op jit(solution)/shard_map/ppermute | solution.py:103
  264.2 2.2 collective-permute-done.16
  268.8 2.9 fusion.98
  271.7 2.5 fusion.206
  277.0 2.6 reshape.357
  281.2 2.7 convolution_add_fusion.23
  283.9 2.3 convolution_add_fusion.22
  286.2 2.3 fusion.52
  288.5 2.3 fusion.51
  293.9 2.5 fusion.49
  297.9 2.1 reshape_squeeze.4
  300.0 2.8 fusion.345
  305.2 2.9 fusion.343
  310.5 3.0 subtract_convert_fusion.3
  318.4 3.6 all-to-all-start.1
  322.0 2.9 fusion.78
  326.8 2.3 fusion.356
  329.1 2.3 fusion.69
  333.9 3.4 all-to-all-done.1
  337.3 3.8 all-to-all-start.2
  341.3 2.3 fusion.353
  343.6 2.5 fusion.70
  348.6 7.8 %all-to-all-done.2 = bf16[8,128,512]{2,1,0:T(8,128)(2,1)S(1)} async-done(((bf16[8,128,512]{2,1,0:T(8,128)(2,1)}), bf16[8,128,512]{2,1,0:T(8,128)(2,1)S(1)}, u32[]{:S(2)}, u32[]{:S(2)}) %all-to-all-start.2) | async-done | bytes 1048608 | tf_op jit(solution)/shard_map/all_to_all | solution.py:241
  356.4 4.2 %all-to-all-start.3 = ((bf16[8,128,512]{2,1,0:T(8,128)(2,1)}), bf16[8,128,512]{2,1,0:T(8,128)(2,1)}, u32[]{:S(2)}, u32[]{:S(2)}) async-start(bf16[8,128,512]{2,1,0:T(8,128)(2,1)} %bitcast.48), calls=%async_computation.3 | async-start | bytes 2097152 | tf_op jit(solution)/shard_map/all_to_all | solution.py:241
  361.6 2.3 fusion.350
  363.9 2.4 fusion.71
  368.8 7.3 %all-to-all-done.3 = bf16[8,128,512]{2,1,0:T(8,128)(2,1)} async-done(((bf16[8,128,512]{2,1,0:T(8,128)(2,1)}), bf16[8,128,512]{2,1,0:T(8,128)(2,1)}, u32[]{:S(2)}, u32[]{:S(2)}) %all-to-all-start.3) | async-done | bytes 1048608 | tf_op jit(solution)/shard_map/all_to_all | solution.py:241
  376.1 3.6 all-to-all-start.4
  382.7 2.8 fusion.62
  385.6 9.4 %all-to-all-done.4 = bf16[8,128,512]{2,1,0:T(8,128)(2,1)S(1)} async-done(((bf16[8,128,512]{2,1,0:T(8,128)(2,1)}), bf16[8,128,512]{2,1,0:T(8,128)(2,1)S(1)}, u32[]{:S(2)}, u32[]{:S(2)}) %all-to-all-start.4) | async-done | bytes 1048608 | tf_op jit(solution)/shard_map/all_to_all | solution.py:241
  397.0 2.4 copy.255
  (280 shorter events, 106.9 us)
Async XLA Ops:
  7.2 34.4 %copy-start.38 = (s32[2]{0:T(128)S(1)}, s32[2]{0:T(128)}, u32[]{:S(2)}) copy-start(s32[2]{0:T(128)} %param.21) | copy-start | bytes 28
  7.2 34.6 %copy-start.14 = (bf16[1024,2,256]{2,1,0:T(2,128)(2,1)S(1)}, bf16[1024,2,256]{2,1,0:T(2,128)(2,1)}, u32[]{:S(2)}) copy-start(bf16[1024,2,256]{2,1,0:T(2,128)(2,1)} %param.29) | copy-start | bytes 3145732
  7.2 35.8 %copy-start.30 = (bf16[2,2,2048]{2,1,0:T(2,128)(2,1)S(1)}, bf16[2,2,2048]{2,1,0:T(2,128)(2,1)}, u32[]{:S(2)}) copy-start(bf16[2,2,2048]{2,1,0:T(2,128)(2,1)} %param.16) | copy-start | bytes 49156
  7.2 154.8 %all-gather.2.cloned.1.call-start = ((), (), s32[]{:S(2)}) async-start(), calls=%async_computation.5 | async-start | bytes 10485760 | tf_op jit(solution)/shard_map/all_gather | solution.py:149
  8.0 42.0 %copy-start.34 = (bf16[2,2,256]{2,1,0:T(2,128)(2,1)S(1)}, bf16[2,2,256]{2,1,0:T(2,128)(2,1)}, u32[]{:S(2)}) copy-start(bf16[2,2,256]{2,1,0:T(2,128)(2,1)} %param.19) | copy-start | bytes 6148
  12.3 27.2 %collective-permute-start.34 = (bf16[1024,512]{1,0:T(8,128)(2,1)}, bf16[1024,512]{1,0:T(8,128)(2,1)}, u32[]{:S(2)}, u32[]{:S(2)}) collective-permute-start(bf16[1024,512]{1,0:T(8,128)(2,1)} %get-tuple-element.27), channel_id=1, source_target_pairs={{0,8},{4,12},{8,0},{12,4},{16,24},{20,28},{24,16},{28,20},{1,9},{5... | collective-permute-start | bytes 3145736 | tf_op jit(solution)/shard_map/ppermute | solution.py:103
  15.2 26.5 %collective-permute-start.36 = (bf16[1024,512]{1,0:T(8,128)(2,1)}, bf16[1024,512]{1,0:T(8,128)(2,1)}, u32[]{:S(2)}, u32[]{:S(2)}) collective-permute-start(bf16[1024,512]{1,0:T(8,128)(2,1)} %get-tuple-element.27), channel_id=1, source_target_pairs={{0,16},{4,20},{8,24},{12,28},{16,0},{20,4},{24,8},{28,12},{1,17},{... | collective-permute-start | bytes 3145736 | tf_op jit(solution)/shard_map/ppermute | solution.py:103
  16.7 45.1 %collective-permute-start.26 = (bf16[1024,512]{1,0:T(8,128)(2,1)}, bf16[1024,512]{1,0:T(8,128)(2,1)S(1)}, u32[]{:S(2)}, u32[]{:S(2)}) collective-permute-start(bf16[1024,512]{1,0:T(8,128)(2,1)} %get-tuple-element.28), channel_id=1, source_target_pairs={{0,8},{4,12},{8,0},{12,4},{16,24},{20,28},{24,16},{28,20},{1,9},{5... | collective-permute-start | bytes 3145736 | tf_op jit(solution)/shard_map/ppermute | solution.py:103
  17.3 46.8 %collective-permute-start.28 = (bf16[1024,512]{1,0:T(8,128)(2,1)}, bf16[1024,512]{1,0:T(8,128)(2,1)}, u32[]{:S(2)}, u32[]{:S(2)}) collective-permute-start(bf16[1024,512]{1,0:T(8,128)(2,1)} %get-tuple-element.28), channel_id=1, source_target_pairs={{0,16},{4,20},{8,24},{12,28},{16,0},{20,4},{24,8},{28,12},{1,17},{... | collective-permute-start | bytes 3145736 | tf_op jit(solution)/shard_map/ppermute | solution.py:103
  17.3 67.1 %collective-permute-start.18 = (bf16[1024,512]{1,0:T(8,128)(2,1)}, bf16[1024,512]{1,0:T(8,128)(2,1)S(1)}, u32[]{:S(2)}, u32[]{:S(2)}) collective-permute-start(bf16[1024,512]{1,0:T(8,128)(2,1)} %get-tuple-element.26), channel_id=1, source_target_pairs={{0,8},{4,12},{8,0},{12,4},{16,24},{20,28},{24,16},{28,20},{1,9},{5... | collective-permute-start | bytes 3145736 | tf_op jit(solution)/shard_map/ppermute | solution.py:103
  20.7 297.7 %all-to-all-start = ((s32[8,1,136]{2,1,0:T(1,128)}), s32[8,1,136]{2,1,0:T(1,128)S(1)}, u32[]{:S(2)}, u32[]{:S(2)}) async-start(s32[8,1,136]{2,1,0:T(1,128)} %reshape.393), calls=%async_computation | async-start | bytes 16384 | tf_op jit(solution)/shard_map/all_to_all | solution.py:181
  39.5 47.1 %collective-permute-start.20 = (bf16[1024,512]{1,0:T(8,128)(2,1)}, bf16[1024,512]{1,0:T(8,128)(2,1)}, u32[]{:S(2)}, u32[]{:S(2)}) collective-permute-start(bf16[1024,512]{1,0:T(8,128)(2,1)} %get-tuple-element.26), channel_id=1, source_target_pairs={{0,16},{4,20},{8,24},{12,28},{16,0},{20,4},{24,8},{28,12},{1,17},{... | collective-permute-start | bytes 3145736 | tf_op jit(solution)/shard_map/ppermute | solution.py:103
  41.7 140.7 %collective-permute-start.9 = (bf16[1024,2048]{1,0:T(8,128)(2,1)}, bf16[1024,2048]{1,0:T(8,128)(2,1)}, u32[]{:S(2)}, u32[]{:S(2)}) collective-permute-start(bf16[1024,2048]{1,0:T(8,128)(2,1)} %param.28), channel_id=1, source_target_pairs={{0,4},{4,0},{8,12},{12,8},{16,20},{20,16},{24,28},{28,24},{1,5},{5... | collective-permute-start | bytes 12582920 | tf_op jit(solution)/shard_map/ppermute | solution.py:103
  43.0 45.4 %copy-start.29 = (f32[8192]{0:T(1024)S(1)}, f32[8192]{0:T(1024)}, u32[]{:S(2)}) copy-start(f32[8192]{0:T(1024)} %param.27) | copy-start | bytes 98308
  43.0 45.5 %copy-start.35 = (bf16[2,2,256]{2,1,0:T(2,128)(2,1)S(1)}, bf16[2,2,256]{2,1,0:T(2,128)(2,1)}, u32[]{:S(2)}) copy-start(bf16[2,2,256]{2,1,0:T(2,128)(2,1)} %param.20) | copy-start | bytes 6148
  50.0 45.9 %copy-start.31 = (f32[2048]{0:T(1024)S(1)}, f32[2048]{0:T(1024)}, u32[]{:S(2)}) copy-start(f32[2048]{0:T(1024)} %param.30) | copy-start | bytes 24580
  53.7 30.6 %copy-start.15 = (f32[2,2,2,8,4096]{4,3,0,2,1:T(8,128)}, f32[2,2,2,8,4096]{4,3,0,2,1:T(8,128)S(1)}, u32[]{:S(2)}) copy-start(f32[2,2,2,8,4096]{4,3,0,2,1:T(8,128)S(1)} %get-tuple-element.66) | copy-start | bytes 3145732
  61.9 51.0 %copy-start.8 = (bf16[1024,512]{1,0:T(8,128)(2,1)}, bf16[1024,512]{1,0:T(8,128)(2,1)S(1)}, u32[]{:S(2)}) copy-start(bf16[1024,512]{1,0:T(8,128)(2,1)S(1)} %collective-permute-done.26) | copy-start | bytes 3145732
  61.9 45.1 %collective-permute-start.10 = (bf16[1024,512]{1,0:T(8,128)(2,1)}, bf16[1024,512]{1,0:T(8,128)(2,1)}, u32[]{:S(2)}, u32[]{:S(2)}) collective-permute-start(bf16[1024,512]{1,0:T(8,128)(2,1)} %get-tuple-element.25), channel_id=1, source_target_pairs={{0,8},{4,12},{8,0},{12,4},{16,24},{20,28},{24,16},{28,20},{1,9},{5... | collective-permute-start | bytes 3145736 | tf_op jit(solution)/shard_map/ppermute | solution.py:103
  64.1 45.0 %collective-permute-start.12 = (bf16[1024,512]{1,0:T(8,128)(2,1)}, bf16[1024,512]{1,0:T(8,128)(2,1)}, u32[]{:S(2)}, u32[]{:S(2)}) collective-permute-start(bf16[1024,512]{1,0:T(8,128)(2,1)} %get-tuple-element.25), channel_id=1, source_target_pairs={{0,16},{4,20},{8,24},{12,28},{16,0},{20,4},{24,8},{28,12},{1,17},{... | collective-permute-start | bytes 3145736 | tf_op jit(solution)/shard_map/ppermute | solution.py:103
  84.4 28.5 %copy-start.6 = (bf16[1024,512]{1,0:T(8,128)(2,1)}, bf16[1024,512]{1,0:T(8,128)(2,1)S(1)}, u32[]{:S(2)}) copy-start(bf16[1024,512]{1,0:T(8,128)(2,1)S(1)} %collective-permute-done.18) | copy-start | bytes 3145732
  84.4 44.2 %collective-permute-start.1 = (bf16[1024,512]{1,0:T(8,128)(2,1)}, bf16[1024,512]{1,0:T(8,128)(2,1)S(1)}, u32[]{:S(2)}, u32[]{:S(2)}) collective-permute-start(bf16[1024,512]{1,0:T(8,128)(2,1)} %bitcast.274), channel_id=1, source_target_pairs={{0,8},{4,12},{8,0},{12,4},{16,24},{20,28},{24,16},{28,20},{1,9},{5... | collective-permute-start | bytes 3145736 | tf_op jit(solution)/shard_map/ppermute | solution.py:103
  86.7 44.9 %collective-permute-start.3 = (bf16[1024,512]{1,0:T(8,128)(2,1)}, bf16[1024,512]{1,0:T(8,128)(2,1)}, u32[]{:S(2)}, u32[]{:S(2)}) collective-permute-start(bf16[1024,512]{1,0:T(8,128)(2,1)} %bitcast.275), channel_id=1, source_target_pairs={{0,16},{4,20},{8,24},{12,28},{16,0},{20,4},{24,8},{28,12},{1,17},{... | collective-permute-start | bytes 3145736 | tf_op jit(solution)/shard_map/ppermute | solution.py:103
  107.0 77.8 %collective-permute-start = (bf16[1024,512]{1,0:T(8,128)(2,1)}, bf16[1024,512]{1,0:T(8,128)(2,1)}, u32[]{:S(2)}, u32[]{:S(2)}) collective-permute-start(bf16[1024,512]{1,0:T(8,128)(2,1)} %bitcast.276), channel_id=1, source_target_pairs={{0,4},{4,0},{8,12},{12,8},{16,20},{20,16},{24,28},{28,24},{1,5},{5... | collective-permute-start | bytes 3145736 | tf_op jit(solution)/shard_map/ppermute | solution.py:103
  109.1 113.2 %collective-permute-start.38 = (bf16[512,512]{1,0:T(8,128)(2,1)}, bf16[512,512]{1,0:T(8,128)(2,1)}, u32[]{:S(2)}, u32[]{:S(2)}) collective-permute-start(bf16[512,512]{1,0:T(8,128)(2,1)} %slice.240), channel_id=1, source_target_pairs={{0,16},{4,20},{8,24},{12,28},{16,0},{20,4},{24,8},{28,12},{1,17},{... | collective-permute-start | bytes 1572872 | tf_op jit(solution)/shard_map/ppermute | solution.py:103
  128.6 38.6 %copy-start.10 = (bf16[1024,512]{1,0:T(8,128)(2,1)}, bf16[1024,512]{1,0:T(8,128)(2,1)S(1)}, u32[]{:S(2)}) copy-start(bf16[1024,512]{1,0:T(8,128)(2,1)S(1)} %collective-permute-done.1) | copy-start | bytes 3145732
  128.6 101.1 %collective-permute-start.40 = (bf16[512,512]{1,0:T(8,128)(2,1)}, bf16[512,512]{1,0:T(8,128)(2,1)}, u32[]{:S(2)}, u32[]{:S(2)}) collective-permute-start(bf16[512,512]{1,0:T(8,128)(2,1)} %slice.241), channel_id=1, source_target_pairs={{0,8},{4,12},{8,0},{12,4},{16,24},{20,28},{24,16},{28,20},{1,9},{5... | collective-permute-start | bytes 1572872 | tf_op jit(solution)/shard_map/ppermute | solution.py:103
  131.6 62.4 %collective-permute-start.5 = (bf16[512,512]{1,0:T(8,128)(2,1)}, bf16[512,512]{1,0:T(8,128)(2,1)}, u32[]{:S(2)}, u32[]{:S(2)}) collective-permute-start(bf16[512,512]{1,0:T(8,128)(2,1)} %slice.211), channel_id=1, source_target_pairs={{0,16},{4,20},{8,24},{12,28},{16,0},{20,4},{24,8},{28,12},{1,17},{... | collective-permute-start | bytes 1572872 | tf_op jit(solution)/shard_map/ppermute | solution.py:103
  182.4 14.6 %collective-permute-start.2 = (bf16[1024,512]{1,0:T(8,128)(2,1)}, bf16[1024,512]{1,0:T(8,128)(2,1)S(1)}, u32[]{:S(2)}, u32[]{:S(2)}) collective-permute-start(bf16[1024,512]{1,0:T(8,128)(2,1)} %copy-done.10), channel_id=1, source_target_pairs={{0,4},{4,0},{8,12},{12,8},{16,20},{20,16},{24,28},{28,24},{1,5},{5... | collective-permute-start | bytes 3145736 | tf_op jit(solution)/shard_map/ppermute | solution.py:103
  184.8 23.2 %collective-permute-start.4 = (bf16[1024,512]{1,0:T(8,128)(2,1)}, bf16[1024,512]{1,0:T(8,128)(2,1)S(1)}, u32[]{:S(2)}, u32[]{:S(2)}) collective-permute-start(bf16[1024,512]{1,0:T(8,128)(2,1)} %collective-permute-done.3), channel_id=1, source_target_pairs={{0,4},{4,0},{8,12},{12,8},{16,20},{20,16},{24,28},{28,24},{1,5},{5... | collective-permute-start | bytes 3145736 | tf_op jit(solution)/shard_map/ppermute | solution.py:103
  194.1 14.0 %collective-permute-start.7 = (bf16[512,512]{1,0:T(8,128)(2,1)S(1)}, bf16[512,512]{1,0:T(8,128)(2,1)S(1)}, u32[]{:S(2)}, u32[]{:S(2)}) collective-permute-start(bf16[512,512]{1,0:T(8,128)(2,1)S(1)} %copy-done.24), channel_id=1, source_target_pairs={{0,8},{4,12},{8,0},{12,4},{16,24},{20,28},{24,16},{28,20},{1,9},{5... | collective-permute-start | bytes 1572872 | tf_op jit(solution)/shard_map/ppermute | solution.py:103
  197.1 44.0 %collective-permute-start.30 = (bf16[512,512]{1,0:T(8,128)(2,1)}, bf16[512,512]{1,0:T(8,128)(2,1)}, u32[]{:S(2)}, u32[]{:S(2)}) collective-permute-start(bf16[512,512]{1,0:T(8,128)(2,1)} %slice.235), channel_id=1, source_target_pairs={{0,16},{4,20},{8,24},{12,28},{16,0},{20,4},{24,8},{28,12},{1,17},{... | collective-permute-start | bytes 1572872 | tf_op jit(solution)/shard_map/ppermute | solution.py:103
  208.0 3.7 collective-permute-start.6
  208.0 4.3 %collective-permute-start.8 = (bf16[512,512]{1,0:T(8,128)(2,1)S(1)}, bf16[512,512]{1,0:T(8,128)(2,1)S(1)}, u32[]{:S(2)}, u32[]{:S(2)}) collective-permute-start(bf16[512,512]{1,0:T(8,128)(2,1)S(1)} %collective-permute-done.7), channel_id=1, source_target_pairs={{0,4},{4,0},{8,12},{12,8},{16,20},{20,16},{24,28},{28,24},{1,5},{5... | collective-permute-start | bytes 1572872 | tf_op jit(solution)/shard_map/ppermute | solution.py:103
  211.7 13.5 %collective-permute-start.35 = (bf16[1024,512]{1,0:T(8,128)(2,1)}, bf16[1024,512]{1,0:T(8,128)(2,1)}, u32[]{:S(2)}, u32[]{:S(2)}) collective-permute-start(bf16[1024,512]{1,0:T(8,128)(2,1)} %collective-permute-done.34), channel_id=1, source_target_pairs={{0,4},{4,0},{8,12},{12,8},{16,20},{20,16},{24,28},{28,24},{1,5},{5... | collective-permute-start | bytes 3145736 | tf_op jit(solution)/shard_map/ppermute | solution.py:103
  212.4 17.4 %collective-permute-start.37 = (bf16[1024,512]{1,0:T(8,128)(2,1)}, bf16[1024,512]{1,0:T(8,128)(2,1)}, u32[]{:S(2)}, u32[]{:S(2)}) collective-permute-start(bf16[1024,512]{1,0:T(8,128)(2,1)} %collective-permute-done.36), channel_id=1, source_target_pairs={{0,4},{4,0},{8,12},{12,8},{16,20},{20,16},{24,28},{28,24},{1,5},{5... | collective-permute-start | bytes 3145736 | tf_op jit(solution)/shard_map/ppermute | solution.py:103
  222.3 21.8 %collective-permute-start.32 = (bf16[512,512]{1,0:T(8,128)(2,1)}, bf16[512,512]{1,0:T(8,128)(2,1)S(1)}, u32[]{:S(2)}, u32[]{:S(2)}) collective-permute-start(bf16[512,512]{1,0:T(8,128)(2,1)} %slice.236), channel_id=1, source_target_pairs={{0,8},{4,12},{8,0},{12,4},{16,24},{20,28},{24,16},{28,20},{1,9},{5... | collective-permute-start | bytes 1572872 | tf_op jit(solution)/shard_map/ppermute | solution.py:103
  225.3 26.8 %collective-permute-start.22 = (bf16[512,512]{1,0:T(8,128)(2,1)}, bf16[512,512]{1,0:T(8,128)(2,1)S(1)}, u32[]{:S(2)}, u32[]{:S(2)}) collective-permute-start(bf16[512,512]{1,0:T(8,128)(2,1)} %slice.229), channel_id=1, source_target_pairs={{0,16},{4,20},{8,24},{12,28},{16,0},{20,4},{24,8},{28,12},{1,17},{... | collective-permute-start | bytes 1572872 | tf_op jit(solution)/shard_map/ppermute | solution.py:103
  229.7 5.1 %collective-permute-start.39 = (bf16[512,512]{1,0:T(8,128)(2,1)}, bf16[512,512]{1,0:T(8,128)(2,1)S(1)}, u32[]{:S(2)}, u32[]{:S(2)}) collective-permute-start(bf16[512,512]{1,0:T(8,128)(2,1)} %collective-permute-done.38), channel_id=1, source_target_pairs={{0,4},{4,0},{8,12},{12,8},{16,20},{20,16},{24,28},{28,24},{1,5},{5... | collective-permute-start | bytes 1572872 | tf_op jit(solution)/shard_map/ppermute | solution.py:103
  229.8 5.6 %collective-permute-start.41 = (bf16[512,512]{1,0:T(8,128)(2,1)}, bf16[512,512]{1,0:T(8,128)(2,1)S(1)}, u32[]{:S(2)}, u32[]{:S(2)}) collective-permute-start(bf16[512,512]{1,0:T(8,128)(2,1)} %collective-permute-done.40), channel_id=1, source_target_pairs={{0,4},{4,0},{8,12},{12,8},{16,20},{20,16},{24,28},{28,24},{1,5},{5... | collective-permute-start | bytes 1572872 | tf_op jit(solution)/shard_map/ppermute | solution.py:103
  234.8 8.4 %collective-permute-start.27 = (bf16[1024,512]{1,0:T(8,128)(2,1)S(1)}, bf16[1024,512]{1,0:T(8,128)(2,1)S(1)}, u32[]{:S(2)}, u32[]{:S(2)}) collective-permute-start(bf16[1024,512]{1,0:T(8,128)(2,1)S(1)} %copy-done.9), channel_id=1, source_target_pairs={{0,4},{4,0},{8,12},{12,8},{16,20},{20,16},{24,28},{28,24},{1,5},{5... | collective-permute-start | bytes 3145736 | tf_op jit(solution)/shard_map/ppermute | solution.py:103
  235.4 9.7 %collective-permute-start.29 = (bf16[1024,512]{1,0:T(8,128)(2,1)}, bf16[1024,512]{1,0:T(8,128)(2,1)S(1)}, u32[]{:S(2)}, u32[]{:S(2)}) collective-permute-start(bf16[1024,512]{1,0:T(8,128)(2,1)} %collective-permute-done.28), channel_id=1, source_target_pairs={{0,4},{4,0},{8,12},{12,8},{16,20},{20,16},{24,28},{28,24},{1,5},{5... | collective-permute-start | bytes 3145736 | tf_op jit(solution)/shard_map/ppermute | solution.py:103
  241.0 14.2 %collective-permute-start.24 = (bf16[512,512]{1,0:T(8,128)(2,1)S(1)}, bf16[512,512]{1,0:T(8,128)(2,1)S(1)}, u32[]{:S(2)}, u32[]{:S(2)}) collective-permute-start(bf16[512,512]{1,0:T(8,128)(2,1)S(1)} %copy-done.23), channel_id=1, source_target_pairs={{0,8},{4,12},{8,0},{12,4},{16,24},{20,28},{24,16},{28,20},{1,9},{5... | collective-permute-start | bytes 1572872 | tf_op jit(solution)/shard_map/ppermute | solution.py:103
  243.3 10.7 %collective-permute-start.19 = (bf16[1024,512]{1,0:T(8,128)(2,1)S(1)}, bf16[1024,512]{1,0:T(8,128)(2,1)S(1)}, u32[]{:S(2)}, u32[]{:S(2)}) collective-permute-start(bf16[1024,512]{1,0:T(8,128)(2,1)S(1)} %copy-done.7), channel_id=1, source_target_pairs={{0,4},{4,0},{8,12},{12,8},{16,20},{20,16},{24,28},{28,24},{1,5},{5... | collective-permute-start | bytes 3145736 | tf_op jit(solution)/shard_map/ppermute | solution.py:103
  244.1 2.9 collective-permute-start.31
  245.1 10.2 %collective-permute-start.21 = (bf16[1024,512]{1,0:T(8,128)(2,1)}, bf16[1024,512]{1,0:T(8,128)(2,1)S(1)}, u32[]{:S(2)}, u32[]{:S(2)}) collective-permute-start(bf16[1024,512]{1,0:T(8,128)(2,1)} %collective-permute-done.20), channel_id=1, source_target_pairs={{0,4},{4,0},{8,12},{12,8},{16,20},{20,16},{24,28},{28,24},{1,5},{5... | collective-permute-start | bytes 3145736 | tf_op jit(solution)/shard_map/ppermute | solution.py:103
  247.0 2.6 collective-permute-start.33
  249.6 14.5 %collective-permute-start.14 = (bf16[512,512]{1,0:T(8,128)(2,1)S(1)}, bf16[512,512]{1,0:T(8,128)(2,1)}, u32[]{:S(2)}, u32[]{:S(2)}) collective-permute-start(bf16[512,512]{1,0:T(8,128)(2,1)S(1)} %copy-done.21), channel_id=1, source_target_pairs={{0,16},{4,20},{8,24},{12,28},{16,0},{20,4},{24,8},{28,12},{1,17},{... | collective-permute-start | bytes 1572872 | tf_op jit(solution)/shard_map/ppermute | solution.py:103
  252.1 14.3 %collective-permute-start.16 = (bf16[512,512]{1,0:T(8,128)(2,1)S(1)}, bf16[512,512]{1,0:T(8,128)(2,1)}, u32[]{:S(2)}, u32[]{:S(2)}) collective-permute-start(bf16[512,512]{1,0:T(8,128)(2,1)S(1)} %copy-done.22), channel_id=1, source_target_pairs={{0,8},{4,12},{8,0},{12,4},{16,24},{20,28},{24,16},{28,20},{1,9},{5... | collective-permute-start | bytes 1572872 | tf_op jit(solution)/shard_map/ppermute | solution.py:103
  253.9 32.2 %collective-permute-start.11 = (bf16[1024,512]{1,0:T(8,128)(2,1)}, bf16[1024,512]{1,0:T(8,128)(2,1)}, u32[]{:S(2)}, u32[]{:S(2)}) collective-permute-start(bf16[1024,512]{1,0:T(8,128)(2,1)} %collective-permute-done.10), channel_id=1, source_target_pairs={{0,4},{4,0},{8,12},{12,8},{16,20},{20,16},{24,28},{28,24},{1,5},{5... | collective-permute-start | bytes 3145736 | tf_op jit(solution)/shard_map/ppermute | solution.py:103
  255.2 11.1 %collective-permute-start.23 = (bf16[512,512]{1,0:T(8,128)(2,1)S(1)}, bf16[512,512]{1,0:T(8,128)(2,1)S(1)}, u32[]{:S(2)}, u32[]{:S(2)}) collective-permute-start(bf16[512,512]{1,0:T(8,128)(2,1)S(1)} %collective-permute-done.22), channel_id=1, source_target_pairs={{0,4},{4,0},{8,12},{12,8},{16,20},{20,16},{24,28},{28,24},{1,5},{5... | collective-permute-start | bytes 1572872 | tf_op jit(solution)/shard_map/ppermute | solution.py:103
  255.3 12.0 %collective-permute-start.25 = (bf16[512,512]{1,0:T(8,128)(2,1)S(1)}, bf16[512,512]{1,0:T(8,128)(2,1)S(1)}, u32[]{:S(2)}, u32[]{:S(2)}) collective-permute-start(bf16[512,512]{1,0:T(8,128)(2,1)S(1)} %collective-permute-done.24), channel_id=1, source_target_pairs={{0,4},{4,0},{8,12},{12,8},{16,20},{20,16},{24,28},{28,24},{1,5},{5... | collective-permute-start | bytes 1572872 | tf_op jit(solution)/shard_map/ppermute | solution.py:103
  264.2 24.3 %collective-permute-start.13 = (bf16[1024,512]{1,0:T(8,128)(2,1)}, bf16[1024,512]{1,0:T(8,128)(2,1)}, u32[]{:S(2)}, u32[]{:S(2)}) collective-permute-start(bf16[1024,512]{1,0:T(8,128)(2,1)} %collective-permute-done.12), channel_id=1, source_target_pairs={{0,4},{4,0},{8,12},{12,8},{16,20},{20,16},{24,28},{28,24},{1,5},{5... | collective-permute-start | bytes 3145736 | tf_op jit(solution)/shard_map/ppermute | solution.py:103
  266.4 25.9 %collective-permute-start.15 = (bf16[512,512]{1,0:T(8,128)(2,1)}, bf16[512,512]{1,0:T(8,128)(2,1)}, u32[]{:S(2)}, u32[]{:S(2)}) collective-permute-start(bf16[512,512]{1,0:T(8,128)(2,1)} %collective-permute-done.14), channel_id=1, source_target_pairs={{0,4},{4,0},{8,12},{12,8},{16,20},{20,16},{24,28},{28,24},{1,5},{5... | collective-permute-start | bytes 1572872 | tf_op jit(solution)/shard_map/ppermute | solution.py:103
  266.4 27.5 %collective-permute-start.17 = (bf16[512,512]{1,0:T(8,128)(2,1)}, bf16[512,512]{1,0:T(8,128)(2,1)}, u32[]{:S(2)}, u32[]{:S(2)}) collective-permute-start(bf16[512,512]{1,0:T(8,128)(2,1)} %collective-permute-done.16), channel_id=1, source_target_pairs={{0,4},{4,0},{8,12},{12,8},{16,20},{20,16},{24,28},{28,24},{1,5},{5... | collective-permute-start | bytes 1572872 | tf_op jit(solution)/shard_map/ppermute | solution.py:103
  292.2 12.9 %copy-start.1 = (f32[16,32,4,128]{3,2,1,0:T(4,128)S(1)}, f32[16,32,4,128]{3,2,1,0:T(4,128)}, u32[]{:S(2)}) copy-start(f32[16,32,4,128]{3,2,1,0:T(4,128)} %reshape.360) | copy-start | bytes 3145732
  310.5 16.3 %copy-start.28 = (bf16[16,32,128,1]{2,1,3,0:T(8,128)(2,1)}, bf16[16,32,128,1]{2,1,3,0:T(8,128)(2,1)S(1)}, u32[]{:S(2)}) copy-start(bf16[16,32,128,1]{2,1,3,0:T(8,128)(2,1)S(1)} %get-tuple-element.47) | copy-start | bytes 393220
  318.4 18.9 %all-to-all-start.1 = ((bf16[8,128,512]{2,1,0:T(8,128)(2,1)}), bf16[8,128,512]{2,1,0:T(8,128)(2,1)S(1)}, u32[]{:S(2)}, u32[]{:S(2)}) async-start(bf16[8,128,512]{2,1,0:T(8,128)(2,1)} %bitcast.30), calls=%async_computation.1 | async-start | bytes 2097152 | tf_op jit(solution)/shard_map/all_to_all | solution.py:241
  329.1 14.5 %copy-start.26 = (bf16[16,32,1,128]{3,2,1,0:T(2,128)(2,1)S(1)}, bf16[16,32,1,128]{3,2,1,0:T(2,128)(2,1)}, u32[]{:S(2)}) copy-start(bf16[16,32,1,128]{3,2,1,0:T(2,128)(2,1)} %get-tuple-element.52) | copy-start | bytes 393220
  337.3 19.2 %all-to-all-start.2 = ((bf16[8,128,512]{2,1,0:T(8,128)(2,1)}), bf16[8,128,512]{2,1,0:T(8,128)(2,1)S(1)}, u32[]{:S(2)}, u32[]{:S(2)}) async-start(bf16[8,128,512]{2,1,0:T(8,128)(2,1)} %bitcast.37), calls=%async_computation.2 | async-start | bytes 2097152 | tf_op jit(solution)/shard_map/all_to_all | solution.py:241
  346.6 17.2 %copy-start.18 = (bf16[16,32,4,64]{3,1,2,0:T(8,128)(2,1)S(1)}, bf16[16,32,4,64]{3,1,2,0:T(8,128)(2,1)}, u32[]{:S(2)}) copy-start(bf16[16,32,4,64]{3,1,2,0:T(8,128)(2,1)} %get-tuple-element.57) | copy-start | bytes 786436
  356.4 19.7 %all-to-all-start.3 = ((bf16[8,128,512]{2,1,0:T(8,128)(2,1)}), bf16[8,128,512]{2,1,0:T(8,128)(2,1)}, u32[]{:S(2)}, u32[]{:S(2)}) async-start(bf16[8,128,512]{2,1,0:T(8,128)(2,1)} %bitcast.48), calls=%async_computation.3 | async-start | bytes 2097152 | tf_op jit(solution)/shard_map/all_to_all | solution.py:241
  376.1 18.9 %all-to-all-start.4 = ((bf16[8,128,512]{2,1,0:T(8,128)(2,1)}), bf16[8,128,512]{2,1,0:T(8,128)(2,1)S(1)}, u32[]{:S(2)}, u32[]{:S(2)}) async-start(bf16[8,128,512]{2,1,0:T(8,128)(2,1)} %bitcast.55), calls=%async_computation.4 | async-start | bytes 2097152 | tf_op jit(solution)/shard_map/all_to_all | solution.py:241
  381.9 14.0 %copy-start.25 = (bf16[512,512]{0,1:T(8,128)(2,1)S(1)}, bf16[512,512]{0,1:T(8,128)(2,1)}, u32[]{:S(2)}) copy-start(bf16[512,512]{0,1:T(8,128)(2,1)} %fusion.56) | copy-start | bytes 1572868
  (26 other events, 211.0 us)
Sparse Core Ops, SparseCore 0:
  9.6 152.3 all-gather.1

commit v2 on v1

--- a/solution.py
+++ b/solution.py
@@ -1,6 +1,8 @@
 import jax
 import jax.numpy as jnp
 from jax import lax
+from jax.experimental import pallas as pl
+from jax.experimental.pallas import tpu as pltpu
 from jax.sharding import PartitionSpec as P
 
 QUERY_HEADS = 64
@@ -74,20 +76,21 @@
 
 
 def attend_responses(query_raw, key_rows, value_rows, table):
-    resp_count, span, kv_width = key_rows.shape
+    resp_count, span, kv_count, _ = key_rows.shape
     heads = query_raw.shape[1] // HEAD_SIZE
     query_rows = rotate_half(query_raw.reshape(resp_count, span, heads, HEAD_SIZE), table).astype(
         jnp.bfloat16
     )
+    query_rows = query_rows.reshape(resp_count, span, kv_count, heads // kv_count, HEAD_SIZE)
     scores = jnp.einsum(
-        "btgd,bsd->bgts", query_rows, key_rows, preferred_element_type=jnp.float32
+        "btkgd,bskd->bkgts", query_rows, key_rows, preferred_element_type=jnp.float32
     ) * HEAD_SIZE ** (-0.5)
     indices = jnp.arange(span, dtype=jnp.int32)
     scores = jnp.where(indices[None, :] <= indices[:, None], scores, -jnp.inf)
     highest = jnp.max(scores, axis=-1, keepdims=True)
     weights = jnp.exp(scores - highest)
     weights = (weights / jnp.sum(weights, axis=-1, keepdims=True)).astype(jnp.bfloat16)
-    output = jnp.einsum("bgts,bsd->btgd", weights, value_rows, preferred_element_type=jnp.float32)
+    output = jnp.einsum("bkgts,bskd->btkgd", weights, value_rows, preferred_element_type=jnp.float32)
     return output.reshape(resp_count, span, heads * HEAD_SIZE).astype(jnp.bfloat16)
 
 
@@ -99,29 +102,287 @@
     return (wide * lax.rsqrt(mean + eps_norm) * gain).astype(jnp.bfloat16)
 
 
-def swap(value, nshard, bit):
-    return lax.ppermute(value, "fsdp", [(i, i ^ bit) for i in range(nshard)])
-
-
-def gather_rows(piece, sibling_piece, nshard):
-    depth = piece.shape[0]
-    half = depth // 2
-    over_x = swap(piece, nshard, 2)
-    over_y = swap(piece, nshard, 4)
-    far_low = swap(over_x[:half], nshard, 4)
-    far_high = swap(over_y[half:], nshard, 2)
-    return [
-        (0, 0, piece),
-        (1, 0, sibling_piece),
-        (2, 0, over_x),
-        (3, 0, swap(over_x, nshard, 1)),
-        (4, 0, over_y),
-        (5, 0, swap(over_y, nshard, 1)),
-        (6, 0, far_low),
-        (7, 0, swap(far_low, nshard, 1)),
-        (6, half, far_high),
-        (7, half, swap(far_high, nshard, 1)),
+MESH = pl.DeviceIdType.MESH
+ROW_PIECES = 4
+TOKEN_PIECES = 2
+COLUMN_TILE = 512
+
+
+def gather_project_kernel(
+    x_ref,
+    wq_ref,
+    wkv_ref,
+    gain_ref,
+    out_ref,
+    wbuf,
+    xbuf,
+    local_sem,
+    x_recv,
+    x_up,
+    x_down,
+    link_recv,
+    pair_recv,
+    send_x,
+    send_y,
+    send_pair,
+):
+    tp_size = xbuf.shape[0]
+    tokens = xbuf.shape[1]
+    depth = wq_ref.shape[0]
+    q_width = wq_ref.shape[1]
+    width = wbuf.shape[2]
+    f = lax.axis_index("fsdp")
+    t = lax.axis_index("tp")
+    core, chip_x, chip_y = f % 2, (f // 2) % 2, f // 4
+    pair = f + 1 - 2 * core
+    over_x = f + 2 - 4 * chip_x
+    over_y = f + 4 - 8 * chip_y
+    has_up, has_down = t < tp_size - 1, t > 0
+
+    own_rows = pl.ds(pl.multiple_of(core * depth, depth), depth)
+    local = [
+        pltpu.make_async_copy(x_ref, xbuf.at[t], local_sem.at[0]),
+        pltpu.make_async_copy(
+            wq_ref, wbuf.at[0, own_rows, pl.ds(0, q_width)], local_sem.at[1]
+        ),
+        pltpu.make_async_copy(
+            wkv_ref, wbuf.at[0, own_rows, pl.ds(q_width, width - q_width)], local_sem.at[2]
+        ),
     ]
+    for copy in local:
+        copy.start()
+
+    barrier = pltpu.get_barrier_semaphore()
+    for other in (pair, over_x, over_y):
+        pl.semaphore_signal(barrier, inc=1, device_id={"fsdp": other}, device_id_type=MESH)
+
+    @pl.when(has_up)
+    def _():
+        pl.semaphore_signal(barrier, inc=1, device_id={"tp": t + 1}, device_id_type=MESH)
+
+    @pl.when(has_down)
+    def _():
+        pl.semaphore_signal(barrier, inc=1, device_id={"tp": t - 1}, device_id_type=MESH)
+
+    @pl.when(has_up & has_down)
+    def _():
+        pl.semaphore_wait(barrier, 5)
+
+    @pl.when(jnp.logical_not(has_up & has_down))
+    def _():
+        pl.semaphore_wait(barrier, 4)
+
+    for copy in local:
+        copy.wait()
+
+    piece_tokens = tokens // TOKEN_PIECES
+
+    def token_copy(block, piece, up):
+        part = xbuf.at[block, pl.ds(piece * piece_tokens, piece_tokens)]
+        return pltpu.make_async_remote_copy(
+            src_ref=part,
+            dst_ref=part,
+            send_sem=(x_up if up else x_down).at[block, piece],
+            recv_sem=x_recv.at[block, piece],
+            device_id={"tp": t + 1 if up else t - 1},
+            device_id_type=MESH,
+        )
+
+    def send_tokens(block, piece, up):
+        @pl.when(has_up if up else has_down)
+        def _():
+            token_copy(block, piece, up).start()
+
+    piece_rows = depth // ROW_PIECES
+
+    def weight_copy(slot, to_slot, piece, send_sem, recv_sem, target):
+        rows = pl.ds(pl.multiple_of(core * depth + piece * piece_rows, piece_rows), piece_rows)
+        return pltpu.make_async_remote_copy(
+            src_ref=wbuf.at[slot, rows],
+            dst_ref=wbuf.at[to_slot, rows],
+            send_sem=send_sem,
+            recv_sem=recv_sem,
+            device_id={"fsdp": target},
+            device_id_type=MESH,
+        )
+
+    def to_pair(slot, piece):
+        return weight_copy(
+            slot, slot, piece, send_pair.at[slot, piece], pair_recv.at[slot, piece], pair
+        )
+
+    def own_x(piece):
+        return weight_copy(0, 1, piece, send_x.at[0, piece], link_recv.at[1, piece], over_x)
+
+    def own_y(piece):
+        return weight_copy(0, 2, piece, send_y.at[0, piece], link_recv.at[2, piece], over_y)
+
+    def relay_x(piece):
+        return weight_copy(2, 3, piece, send_x.at[1, piece], link_recv.at[3, piece], over_x)
+
+    def relay_y(piece):
+        return weight_copy(1, 3, piece, send_y.at[1, piece], link_recv.at[3, piece], over_y)
+
+    half = ROW_PIECES // 2
+    order_x = list(range(ROW_PIECES))
+    order_y = order_x[half:] + order_x[:half]
+    for piece in range(TOKEN_PIECES):
+        send_tokens(t, piece, True)
+        send_tokens(t, piece, False)
+    for px, py in zip(order_x, order_y):
+        own_x(px).start()
+        own_y(py).start()
+    for piece in range(ROW_PIECES):
+        to_pair(0, piece).start()
+
+    def weights_arrive(step):
+        px, py = order_x[step], order_y[step]
+        own_x(px).wait_recv()
+        if px < half:
+            relay_y(px).start()
+        to_pair(1, px).start()
+        own_y(py).wait_recv()
+        if py >= half:
+            relay_x(py).start()
+        to_pair(2, py).start()
+
+    def tokens_arrive(step, forward):
+        for piece in range(TOKEN_PIECES):
+
+            @pl.when(t - step >= 0)
+            def _():
+                token_copy(t - step, piece, True).wait_recv()
+                if forward:
+                    send_tokens(t - step, piece, True)
+
+            @pl.when(t + step < tp_size)
+            def _():
+                token_copy(t + step, piece, False).wait_recv()
+                if forward:
+                    send_tokens(t + step, piece, False)
+
+    weights_arrive(0)
+    tokens_arrive(1, tp_size > 2)
+    weights_arrive(1)
+    weights_arrive(2)
+    tokens_arrive(2, tp_size > 3)
+    weights_arrive(3)
+    for step in range(3, tp_size):
+        tokens_arrive(step, step < tp_size - 1)
+
+    def far_arrive(piece):
+        (relay_y if piece < half else relay_x)(piece).wait_recv()
+        to_pair(3, piece).start()
+
+    far_arrive(order_x[0])
+    far_arrive(order_y[0])
+
+    for block in range(tp_size):
+        for piece in range(TOKEN_PIECES):
+
+            @pl.when(has_up & (t >= block))
+            def _():
+                token_copy(block, piece, True).wait_send()
+
+            @pl.when(has_down & (t <= block))
+            def _():
+                token_copy(block, piece, False).wait_send()
+
+    strip = 16
+    features = tp_size * xbuf.shape[2]
+
+    def normalize_strip(i, carry):
+        rows = pl.ds(pl.multiple_of(i * strip, strip), strip)
+        squares = jnp.zeros((strip, 1), jnp.float32)
+        for block in range(tp_size):
+            wide = xbuf[block, rows, :].astype(jnp.float32)
+            squares += jnp.sum(wide * wide, axis=1, keepdims=True)
+        scale = lax.rsqrt(squares / features + eps_norm)
+        for block in range(tp_size):
+            wide = xbuf[block, rows, :].astype(jnp.float32)
+            xbuf[block, rows, :] = (wide * scale * gain_ref[block : block + 1, :]).astype(
+                jnp.bfloat16
+            )
+        return carry
+
+    lax.fori_loop(0, tokens // strip, normalize_strip, 0)
+
+    def chip_of(slot):
+        return 2 * ((chip_y + slot // 2) % 2) + (chip_x + slot % 2) % 2
+
+    def product(slot, columns):
+        return jnp.dot(
+            xbuf[chip_of(slot)], wbuf[slot, :, columns], preferred_element_type=jnp.float32
+        )
+
+    def tile(i):
+        return pl.ds(pl.multiple_of(i * COLUMN_TILE, COLUMN_TILE), COLUMN_TILE)
+
+    for slot in range(3):
+        for piece in range(ROW_PIECES):
+            to_pair(slot, piece).wait_recv()
+
+    def near_tile(i, carry):
+        columns = tile(i)
+        out_ref[:, columns] = product(0, columns) + product(1, columns) + product(2, columns)
+        return carry
+
+    lax.fori_loop(0, width // COLUMN_TILE, near_tile, 0)
+
+    far_arrive(order_x[1])
+    far_arrive(order_y[1])
+    for piece in range(ROW_PIECES):
+        to_pair(3, piece).wait_recv()
+
+    def far_tile(i, carry):
+        columns = tile(i)
+        out_ref[:, columns] += product(3, columns)
+        return carry
+
+    lax.fori_loop(0, width // COLUMN_TILE, far_tile, 0)
+
+    for piece in range(ROW_PIECES):
+        own_x(piece).wait_send()
+        own_y(piece).wait_send()
+        (relay_y if piece < half else relay_x)(piece).wait_send()
+        for slot in range(4):
+            to_pair(slot, piece).wait_send()
+
+
+def gather_project(x, w_q, w_pairs, norm_gain):
+    tp_size = lax.axis_size("tp")
+    tokens, features = x.shape
+    depth = w_q.shape[0]
+    width = w_q.shape[1] + w_pairs.shape[1]
+    dma = pltpu.SemaphoreType.DMA
+    return pl.pallas_call(
+        gather_project_kernel,
+        out_shape=jax.ShapeDtypeStruct((tokens, width), jnp.float32),
+        in_specs=[pl.BlockSpec(memory_space=pl.ANY)] * 3
+        + [pl.BlockSpec(memory_space=pltpu.VMEM)],
+        out_specs=pl.BlockSpec(memory_space=pltpu.VMEM),
+        scratch_shapes=[
+            pltpu.VMEM((4, 2 * depth, width), jnp.bfloat16),
+            pltpu.VMEM((tp_size, tokens, features), jnp.bfloat16),
+            dma((3,)),
+            dma((tp_size, TOKEN_PIECES)),
+            dma((tp_size, TOKEN_PIECES)),
+            dma((tp_size, TOKEN_PIECES)),
+            dma((4, ROW_PIECES)),
+            dma((4, ROW_PIECES)),
+            dma((2, ROW_PIECES)),
+            dma((2, ROW_PIECES)),
+            dma((4, ROW_PIECES)),
+        ],
+        compiler_params=pltpu.CompilerParams(
+            collective_id=0, has_side_effects=True, vmem_limit_bytes=60 * 1024 * 1024
+        ),
+        cost_estimate=pl.CostEstimate(
+            flops=2 * tokens * features * tp_size * width,
+            bytes_accessed=tokens * features * 2 + depth * width * 2 + tokens * width * 4,
+            transcendentals=0,
+        ),
+    )(x, w_q, w_pairs, norm_gain.reshape(tp_size, features))
 
 
 def on_device(
@@ -143,27 +404,28 @@
     key_value_bias,
 ):
     nshard = lax.axis_size("fsdp")
-    me = lax.axis_index("fsdp")
     resp_count, resp_span, feature_width = resp_embed.shape
     packed_len = resp_count * resp_span
-    full_rows = lax.all_gather(
-        resp_embed.reshape(packed_len, feature_width), "tp", axis=0, tiled=False
-    )
+    own_rows = resp_embed.reshape(packed_len, feature_width)
     pair_width = key_value_weight.shape[1] * key_value_weight.shape[2]
     kv_width = pair_width // 2
     kv_count = kv_width // HEAD_SIZE
     w_pairs = key_value_weight.reshape(key_value_weight.shape[0], pair_width)
     q_width = w_q.shape[1]
-    chunk = (QUERY_HEADS // KEY_VALUE_HEADS) * HEAD_SIZE // 2
-    pieces = [w_pairs] + [w_q[:, i : i + chunk] for i in range(0, q_width, chunk)]
-    if nshard == 8:
-        sibling_q = swap(w_q, nshard, 1)
-        sibling_pieces = [swap(w_pairs, nshard, 1)] + [
-            sibling_q[:, i : i + chunk] for i in range(0, q_width, chunk)
-        ]
-        gathered = [gather_rows(p, s, nshard) for p, s in zip(pieces, sibling_pieces)]
+    if nshard == 8 and w_q.shape[0] * 2 == feature_width:
+        raw = gather_project(own_rows, w_q, w_pairs, norm_gain)
+        query_raw, pair_raw = raw[:, :q_width], raw[:, q_width:]
     else:
-        gathered = [[(0, 0, lax.all_gather(p, "fsdp", axis=0, tiled=True))] for p in pieces]
+        normed = normalize(lax.all_gather(own_rows, "tp", axis=0, tiled=False), norm_gain)
+        normed = jnp.swapaxes(normed, 0, 1).reshape(packed_len, -1)
+        query_raw, pair_raw = (
+            jnp.dot(
+                normed,
+                lax.all_gather(w, "fsdp", axis=0, tiled=True),
+                preferred_element_type=jnp.float32,
+            )
+            for w in (w_q, w_pairs)
+        )
 
     decode_out = decode_local(
         dec_queries, cache_keys, cached_value_rows, step_keys, step_values, prompt_lengths
@@ -195,55 +457,23 @@
     ) - 1
     picks = picks.astype(jnp.bfloat16)
 
-    normed = normalize(full_rows, norm_gain)
-    block_rows = w_q.shape[0]
-    if nshard == 8:
-        per_block = feature_width // block_rows
-        sources = []
-        for bits in range(nshard):
-            owner = jnp.bitwise_xor(me, bits)
-            sources.append(
-                lax.dynamic_slice(
-                    normed,
-                    (owner // per_block, 0, (owner % per_block) * block_rows),
-                    (1, packed_len, block_rows),
-                )[0]
-            )
-    else:
-        sources = [jnp.swapaxes(normed, 0, 1).reshape(packed_len, -1)]
-
-    def project(blocks):
-        total = None
-        for bits, first, rows in blocks:
-            columns = lax.slice_in_dim(sources[bits], first, first + rows.shape[0], axis=1)
-            part = jnp.dot(columns, rows, preferred_element_type=jnp.float32)
-            total = part if total is None else total + part
-        return total
-
     table = rotary_table(resp_span)
-    pair_raw = project(gathered[0]).reshape(packed_len, 2, kv_width) + key_value_bias[None]
+    pair_raw = pair_raw.reshape(packed_len, 2, kv_width) + key_value_bias[None]
     ref_keys = rotate_half(
         pair_raw[:, 0].reshape(resp_count, resp_span, kv_count, HEAD_SIZE), table
     ).astype(jnp.bfloat16)
     ref_values = (
         pair_raw[:, 1].reshape(resp_count, resp_span, kv_count, HEAD_SIZE).astype(jnp.bfloat16)
     )
+    attn = attend_responses(query_raw + bias_q[None, :], ref_keys, ref_values, table)
     spread = jnp.swapaxes(placing.reshape(resp_count, slot_total), 0, 1).astype(jnp.bfloat16)
-    results = []
-    for i, blocks in enumerate(gathered[1:]):
-        query_raw = project(blocks) + bias_q[None, i * chunk : (i + 1) * chunk]
-        kv_head = i // 2
-        attn = attend_responses(query_raw, ref_keys[:, :, kv_head], ref_values[:, :, kv_head], table)
-        slots = jnp.einsum(
-            "sk,krx->srx", spread, attn, preferred_element_type=jnp.float32
-        ).astype(jnp.bfloat16)
-        slots = slots.reshape(nshard, capacity * resp_span, chunk)
-        arrived = lax.all_to_all(slots, "fsdp", split_axis=0, concat_axis=0, tiled=True)
-        arrived = arrived.reshape(slot_total * resp_span, chunk)
-        results.append(
-            jnp.dot(picks, arrived, preferred_element_type=jnp.float32).astype(jnp.bfloat16)
-        )
-    ref_attn = jnp.concatenate(results, axis=1)
+    slots = jnp.einsum(
+        "sk,krx->srx", spread, attn, preferred_element_type=jnp.float32
+    ).astype(jnp.bfloat16)
+    slots = slots.reshape(nshard, capacity * resp_span, q_width)
+    arrived = lax.all_to_all(slots, "fsdp", split_axis=0, concat_axis=0, tiled=True)
+    arrived = arrived.reshape(slot_total * resp_span, q_width)
+    ref_attn = jnp.dot(picks, arrived, preferred_element_type=jnp.float32).astype(jnp.bfloat16)
     return (decode_out, packed_ids, ref_attn)
 
 

time: 413 us -> 291 us (0.70); the launches traced: 407 us -> 290 us
  Pallas kernels: 0 us -> 189 us
  waiting for transfers between devices: 134 us -> 26.2 us
  matrix products: 108 us -> 17.7 us
  starting transfers between devices: 54.1 us -> 9.86 us
  local copies, waits for them, and re-layouts: 71.8 us -> 36.4 us
  between operations: 16.2 us -> 0.92 us
  other arithmetic: 23.4 us -> 10 us
    pallas_call x0 -> x1, Pallas kernels: none -> 189 us  [gather_project(): pl.pallas_call(gather_project_kernel, out_shape=jax.ShapeDtypeStruct((tok...]
    dot_general x54 -> x2, matrix products: 85 us -> 4.25 us  [the longest x1 3.47 us: attend_responses(): jnp.einsum('btkgd,bskd->bkgts', query_rows, key_rows, preferred_element_t...]
    ppermute x42 -> x0, waiting for transfers between devices: 77.9 us -> none  [swap(): return lax.ppermute(value, 'fsdp', [(i, i ^ bit) for i in range(nshard)])]
    ppermute x42 -> x0, starting transfers between devices: 35.6 us -> none  [swap(): return lax.ppermute(value, 'fsdp', [(i, i ^ bit) for i in range(nshard)])]
    all_gather x1 -> x0, waiting for transfers between devices: 27.1 us -> none  [on_device(): lax.all_gather(resp_embed.reshape(packed_len, feature_width), 'tp', axis=...]
    slice x13 -> x1, local copies, waits for them, and re-layouts: 21.4 us -> 1.44 us  [on_device(): query_raw, pair_raw = (raw[:, :q_width], raw[:, q_width:])]
    all_to_all x4 -> x1, starting transfers between devices: 15.2 us -> 4.69 us  [on_device(): lax.all_to_all(slots, 'fsdp', split_axis=0, concat_axis=0, tiled=True)]
    convert_element_type x1 -> x0, other arithmetic: 10.3 us -> none  [normalize(): return (wide * lax.rsqrt(mean + eps_norm) * gain).astype(jnp.bfloat16)]
  transfers between devices with their start and end apart: 48 -> 2, of which waited for: 19 -> 1; matrix products, arithmetic and copies ran while one was open for 49% -> 18% of each run, Pallas kernels for 0% -> 65%
where the time goes in v2:
time: 291 us; the launch traced here: 290 us
  Pallas kernels  189 us (65%)
  local copies, waits for them, and re-layouts  36.4 us (13%)
  waiting for transfers between devices  26.2 us (9%)
  matrix products  17.7 us (6%)
  other arithmetic  10 us (3%)
  starting transfers between devices  9.86 us (3%)
    pallas_call x1, Pallas kernels, gather_project(): pl.pallas_call(gather_project_kernel, out_shape=jax.ShapeDtypeStruct((tok...  189 us
    all_to_all x1, waiting for transfers between devices, on_device(): lax.all_to_all(slots, 'fsdp', split_axis=0, concat_axis=0, tiled=True)  26.2 us
    reshape x1, local copies, waits for them, and re-layouts, decode_local(): key_matrix = cache_keys.reshape(row_count, length, kv_local, HEAD_SIZE)  6.94 us
    reshape x1, local copies, waits for them, and re-layouts, decode_local(): cached_value_rows.reshape(row_count, length, kv_local, HEAD_SIZE)  6.92 us
    dot_general x1, matrix products, on_device(): jnp.dot(picks, arrived, preferred_element_type=jnp.float32)  5.85 us
  transfers between devices with their start and end apart: 2, of which 1 were waited for; matrix products, arithmetic and copies ran while one was open for 18% of the time, Pallas kernels for 65%

profile of v2, /device:TPU:0, one launch (start us, length us, event | category | flops | bytes accessed | tf_op | source)
XLA Modules:
  0.0 290.2 jit_solution(9094127772067344342)
XLA Ops:
  0.6 0.9 convert_reduce_fusion
  1.5 0.7 iota_compare_fusion.4
  2.2 0.1 copy.101
  2.3 0.7 copy.102
  3.1 0.7 copy.103
  3.8 0.8 pad_add_fusion
  4.6 0.1 select_reduce_fusion.1
  4.7 0.7 reshape.325
  5.4 5.2 %all-to-all-start = ((s32[8,1,136]{2,1,0:T(1,128)}), s32[8,1,136]{2,1,0:T(1,128)S(1)}, u32[]{:S(2)}, u32[]{:S(2)}) async-start(s32[8,1,136]{2,1,0:T(1,128)} %reshape.325), calls=%async_computation | async-start | bytes 16384 | tf_op jit(solution)/shard_map/all_to_all | solution.py:443
  10.6 1.4 reshape.298.gain_ref
  12.0 2.4 copy.140
  14.4 189.0 %shard_map.175 = f32[512,2560]{1,0:T(8,128)} custom-call(bf16[512,2048]{1,0:T(8,128)(2,1)} %bitcast.81, bf16[1024,2048]{1,0:T(8,128)(2,1)} %wq_ref.1, bf16[1024,512]{1,0:T(8,128)(2,1)} %bitcast.72, f32[4,2048]{1,0:T(4,128)} %reshape.298.gain_ref), custom_call_target="tpu_custom_call" | custom-call | flops 21474836480 | bytes 12582912 | tf_op jit(solution)/shard_map/pallas_call | solution.py:358
  203.4 0.0 copy-start
  203.4 0.0 copy-start.3
  203.4 1.4 slice.43
  204.9 0.0 copy-done.4
  204.9 0.1 bitcast_add_fusion
  205.1 1.2 copy-done
  206.2 0.0 copy-done.3
  206.2 0.5 add_bitcast_fusion
  206.8 0.9 copy.141
  207.7 0.1 multiply_cosine_fusion
  207.9 2.8 subtract_convert_fusion
  210.7 0.5 copy.108
  211.2 0.3 reshape_squeeze.4
  211.5 0.1 convert_element_type.72
  211.6 0.6 fusion.48
  212.2 2.1 copy.109
  214.3 0.2 subtract_convert_fusion.1
  214.5 3.5 %fusion.7 = f32[16,2,32,32,8]{3,2,4,1,0:T(8,128)S(1)} fusion(bf16[16,32,2,8,64]{4,1,3,2,0:T(8,128)(2,1)S(1)} %bitcast.67, bf16[16,32,2,8,64]{4,1,3,2,0:T(8,128)(2,1)S(1)} %bitcast.66, bf16[16,32,2,64]{3,1,2,0:T(8,128)(2,1)S(1)} %get-tuple-element.8, bf16[16,32,2,64]{3,1,2,0:T(8,128)(2,1)S(1)} %get-tuple-element.7), kind=kOutput, calls=%fused_computation.16 | convolution fusion | flops 71827456 | bytes 3407872 | tf_op jit(solution)/shard_map/btkgd,bskd->bkgts/dot_general | solution.py:85
  218.0 1.5 fusion.51
  219.5 0.8 convert_bitcast_fusion
  220.3 0.8 copy.135
  221.1 2.3 reshape.310
  223.4 2.8 convolution_convert_fusion
  226.2 4.3 %copy.115 = bf16[32,32,2048]{2,1,0:T(8,128)(2,1)} copy(bf16[32,32,2048]{2,0,1:T(8,128)(2,1)S(1)} %convolution_convert_fusion) | data formatting | bytes 8388608 | tf_op jit(solution)/shard_map/convert_element_type | solution.py:472
  230.5 0.0 all-to-all-done
  230.5 4.7 %all-to-all-start.1 = ((bf16[8,128,2048]{2,1,0:T(8,128)(2,1)}), bf16[8,128,2048]{2,1,0:T(8,128)(2,1)}, u32[]{:S(2)}, u32[]{:S(2)}) async-start(bf16[8,128,2048]{2,1,0:T(8,128)(2,1)} %bitcast.65), calls=%async_computation.1 | async-start | bytes 8388608 | tf_op jit(solution)/shard_map/all_to_all | solution.py:474
  235.2 0.0 copy-done.5
  235.2 0.0 copy-done.6
  235.2 0.0 copy-done.2
  235.3 0.1 add.80
  235.3 6.9 %reshape.290 = bf16[2,4096,2,128]{3,2,1,0:T(2,128)(2,1)} reshape(bf16[2,4096,256]{2,1,0:T(8,128)(2,1)} %param.17) | data formatting | bytes 8388608 | tf_op jit(solution)/shard_map/reshape | solution.py:47
  242.3 6.9 %reshape.293 = bf16[2,4096,2,128]{3,2,1,0:T(2,128)(2,1)} reshape(bf16[2,4096,256]{2,1,0:T(8,128)(2,1)} %param.18) | data formatting | bytes 8388608 | tf_op jit(solution)/shard_map/reshape | solution.py:48
  249.2 0.2 fusion.50
  249.4 0.1 iota_compare_fusion.1
  249.5 3.6 %fusion.49 = (f32[2,2,2,8]{3,0,2,1:T(2,128)S(1)}, f32[2,2,2,8,4096]{4,3,0,2,1:T(8,128)S(1)}) fusion(bf16[2,2,2,8,128]{4,3,2,1,0:T(8,128)(2,1)S(1)} %reshape.291, bf16[2,4096,2,128,1]{3,2,1,0,4:T(2,128)(2,1)} %bitcast.70, pred[2,4096]{1,0:T(4,128)(4,1)S(1)} %iota_compare_fusion.1), kind=kOutput, calls=%fused_computation.84 | convolution fusion | flops 67895232 | bytes 5267712 | tf_op jit(solution)/shard_map/srkgd,rckd->srkgc/dot_general | solution.py:52
  253.2 0.3 fusion.30
  253.5 0.2 fusion.40
  253.7 0.0 copy-done.1
  253.7 0.7 fusion.23
  254.5 0.6 convert_element_type.70
  255.1 0.5 broadcast.182
  255.6 0.7 reduce.12
  256.3 0.1 reshape.326
  256.4 0.1 add.84
  256.5 0.2 slice_reduce_fusion
  256.6 0.2 broadcast_reduce_fusion
  256.8 0.1 lt.55
  256.9 0.1 add.78
  257.0 0.5 select_reduce_fusion
  257.5 0.6 broadcast_add_fusion
  258.1 26.2 %all-to-all-done.1 = bf16[8,128,2048]{2,1,0:T(8,128)(2,1)} async-done(((bf16[8,128,2048]{2,1,0:T(8,128)(2,1)}), bf16[8,128,2048]{2,1,0:T(8,128)(2,1)}, u32[]{:S(2)}, u32[]{:S(2)}) %all-to-all-start.1) | async-done | bytes 4194336 | tf_op jit(solution)/shard_map/all_to_all | solution.py:474
  284.3 5.8 %convolution_convert_fusion.1 = bf16[512,2048]{1,0:T(8,128)(2,1)} fusion(bf16[1024,2048]{1,0:T(8,128)(2,1)} %bitcast.21, s32[1024]{0:T(1024)S(1)} %add.81, pred[1024]{0:T(1024)(128)(4,1)S(1)} %lt.56), kind=kOutput, calls=%fused_computation.15 | convolution fusion | flops 2149580800 | bytes 6296576 | tf_op jit(solution)/shard_map/dot_general | solution.py:476
  (27 shorter events, 0.2 us)
Async XLA Ops:
  5.4 225.1 %all-to-all-start = ((s32[8,1,136]{2,1,0:T(1,128)}), s32[8,1,136]{2,1,0:T(1,128)S(1)}, u32[]{:S(2)}, u32[]{:S(2)}) async-start(s32[8,1,136]{2,1,0:T(1,128)} %reshape.325), calls=%async_computation | async-start | bytes 16384 | tf_op jit(solution)/shard_map/all_to_all | solution.py:443
  14.4 190.5 %copy-start.4 = (f32[2,256]{1,0:T(2,128)S(1)}, f32[2,256]{1,0:T(2,128)}, u32[]{:S(2)}) copy-start(f32[2,256]{1,0:T(2,128)} %param.31) | copy-start | bytes 6148
  203.4 2.8 copy-start
  203.4 2.8 copy-start.3
  230.5 4.7 %copy-start.5 = (bf16[2,2,256]{2,1,0:T(2,128)(2,1)S(1)}, bf16[2,2,256]{2,1,0:T(2,128)(2,1)}, u32[]{:S(2)}) copy-start(bf16[2,2,256]{2,1,0:T(2,128)(2,1)} %param.19) | copy-start | bytes 6148
  230.5 4.7 %copy-start.6 = (bf16[2,2,256]{2,1,0:T(2,128)(2,1)S(1)}, bf16[2,2,256]{2,1,0:T(2,128)(2,1)}, u32[]{:S(2)}) copy-start(bf16[2,2,256]{2,1,0:T(2,128)(2,1)} %param.20) | copy-start | bytes 6148
  230.5 4.8 %copy-start.2 = (bf16[2,2,2048]{2,1,0:T(2,128)(2,1)S(1)}, bf16[2,2,2048]{2,1,0:T(2,128)(2,1)}, u32[]{:S(2)}) copy-start(bf16[2,2,2048]{2,1,0:T(2,128)(2,1)} %param.16) | copy-start | bytes 49156
  230.5 53.8 %all-to-all-start.1 = ((bf16[8,128,2048]{2,1,0:T(8,128)(2,1)}), bf16[8,128,2048]{2,1,0:T(8,128)(2,1)}, u32[]{:S(2)}, u32[]{:S(2)}) async-start(bf16[8,128,2048]{2,1,0:T(8,128)(2,1)} %bitcast.65), calls=%async_computation.1 | async-start | bytes 8388608 | tf_op jit(solution)/shard_map/all_to_all | solution.py:474
  242.3 7.1 %copy-start.7 = (s32[2]{0:T(128)S(1)}, s32[2]{0:T(128)}, u32[]{:S(2)}) copy-start(s32[2]{0:T(128)} %param.21) | copy-start | bytes 28
  249.2 4.5 %copy-start.1 = (bf16[2,4096,2,128]{3,2,1,0:T(2,128)(2,1)S(1)}, bf16[2,4096,2,128]{3,2,1,0:T(2,128)(2,1)}, u32[]{:S(2)}) copy-start(bf16[2,4096,2,128]{3,2,1,0:T(2,128)(2,1)} %reshape.293) | copy-start | bytes 12582916

commit v3 on v2

--- a/solution.py
+++ b/solution.py
@@ -1,4 +1,7 @@
+import functools
+
 import jax
+import numpy as np
 import jax.numpy as jnp
 from jax import lax
 from jax.experimental import pallas as pl
@@ -12,27 +15,6 @@
 
 rope_base = 1000000.0
 eps_norm = 1e-06
-
-
-def rotary_table(span):
-    half_dim = HEAD_SIZE // 2
-    frequency = rope_base ** (-jnp.arange(half_dim, dtype=jnp.float32) * 2.0 / HEAD_SIZE)
-    angles = jnp.arange(span, dtype=jnp.int32).astype(jnp.float32)[:, None] * frequency[None, :]
-    return jnp.cos(angles)[None, :, None, :], jnp.sin(angles)[None, :, None, :]
-
-
-def rotate_half(values, table):
-    cosine, sine_part = table
-    half_dim = HEAD_SIZE // 2
-    lower_half = values[..., :half_dim]
-    upper_half = values[..., half_dim:]
-    return jnp.concatenate(
-        [
-            lower_half * cosine - upper_half * sine_part,
-            upper_half * cosine + lower_half * sine_part,
-        ],
-        axis=-1,
-    )
 
 
 def decode_local(
@@ -75,23 +57,104 @@
     return output.reshape(step_count, row_count, head_width).astype(jnp.bfloat16)
 
 
-def attend_responses(query_raw, key_rows, value_rows, table):
-    resp_count, span, kv_count, _ = key_rows.shape
-    heads = query_raw.shape[1] // HEAD_SIZE
-    query_rows = rotate_half(query_raw.reshape(resp_count, span, heads, HEAD_SIZE), table).astype(
-        jnp.bfloat16
-    )
-    query_rows = query_rows.reshape(resp_count, span, kv_count, heads // kv_count, HEAD_SIZE)
-    scores = jnp.einsum(
-        "btkgd,bskd->bkgts", query_rows, key_rows, preferred_element_type=jnp.float32
-    ) * HEAD_SIZE ** (-0.5)
-    indices = jnp.arange(span, dtype=jnp.int32)
-    scores = jnp.where(indices[None, :] <= indices[:, None], scores, -jnp.inf)
-    highest = jnp.max(scores, axis=-1, keepdims=True)
-    weights = jnp.exp(scores - highest)
-    weights = (weights / jnp.sum(weights, axis=-1, keepdims=True)).astype(jnp.bfloat16)
-    output = jnp.einsum("bkgts,bskd->btkgd", weights, value_rows, preferred_element_type=jnp.float32)
-    return output.reshape(resp_count, span, heads * HEAD_SIZE).astype(jnp.bfloat16)
+def attend_kernel(
+    span, slot_resp, q_ref, k_ref, v_ref, bias_q_ref, bias_kv_ref, cos_ref, sin_ref, out_ref, attn
+):
+    tokens, q_width = q_ref.shape
+    heads = q_width // HEAD_SIZE
+    group = 128
+    cosine = jnp.concatenate([cos_ref[...]] * (group // span), axis=0)
+    sine_part = jnp.concatenate([sin_ref[...]] * (group // span), axis=0)
+
+    def rotate(values):
+        turned = pltpu.roll(values, HEAD_SIZE // 2, 1)
+        return (values * cosine + turned * sine_part).astype(jnp.bfloat16)
+
+    row = lax.broadcasted_iota(jnp.int32, (group, group), 0)
+    column = lax.broadcasted_iota(jnp.int32, (group, group), 1)
+    allowed = (row // span == column // span) & (column <= row)
+    allowed = jnp.concatenate([allowed.astype(jnp.float32)] * heads, axis=0) > 0.5
+
+    def one_group(g, carry):
+        rows = pl.ds(pl.multiple_of(g * group, group), group)
+        keys = rotate(k_ref[rows, :] + bias_kv_ref[0:1, :])
+        values = (v_ref[rows, :] + bias_kv_ref[1:2, :]).astype(jnp.bfloat16)
+        queries = jnp.concatenate(
+            [
+                rotate(
+                    q_ref[rows, h * HEAD_SIZE : (h + 1) * HEAD_SIZE]
+                    + bias_q_ref[0:1, h * HEAD_SIZE : (h + 1) * HEAD_SIZE]
+                )
+                for h in range(heads)
+            ],
+            axis=0,
+        )
+        scores = lax.dot_general(
+            queries, keys, (((1,), (1,)), ((), ())), preferred_element_type=jnp.float32
+        ) * HEAD_SIZE ** (-0.5)
+        scores = jnp.where(allowed, scores, -jnp.inf)
+        weights = jnp.exp(scores - jnp.max(scores, axis=1, keepdims=True))
+        weights = (weights / jnp.sum(weights, axis=1, keepdims=True)).astype(jnp.bfloat16)
+        output = jnp.dot(weights, values, preferred_element_type=jnp.float32)
+        output = output.astype(jnp.bfloat16)
+        for h in range(heads):
+            attn[rows, h * HEAD_SIZE : (h + 1) * HEAD_SIZE] = output[h * group : (h + 1) * group]
+        return carry
+
+    lax.fori_loop(0, tokens // group, one_group, 0)
+
+    def one_slot(s, carry):
+        source = pl.ds(pl.multiple_of(slot_resp[s] * span, span), span)
+        out_ref[pl.ds(pl.multiple_of(s * span, span), span), :] = attn[source, :]
+        return carry
+
+    lax.fori_loop(0, out_ref.shape[0] // span, one_slot, 0)
+
+
+def attend_responses(raw, slot_resp, bias_q, key_value_bias, span):
+    tokens = raw.shape[0]
+    q_width = bias_q.shape[0]
+    kv_count = key_value_bias.shape[1] // HEAD_SIZE
+    per_kv = q_width // kv_count
+    first_key = q_width // HEAD_SIZE
+    slot_total = slot_resp.shape[0]
+    half_dim = HEAD_SIZE // 2
+    frequency = np.float32(rope_base) ** (
+        -np.arange(half_dim, dtype=np.float32) * np.float32(2.0 / HEAD_SIZE)
+    )
+    angles = np.arange(span, dtype=np.float32)[:, None] * frequency.astype(np.float32)[None, :]
+    cosine, sine_part = np.cos(angles), np.sin(angles)
+    cosine = np.concatenate([cosine, cosine], axis=1).astype(np.float32)
+    sine_part = np.concatenate([-sine_part, sine_part], axis=1).astype(np.float32)
+    table = pl.BlockSpec((span, HEAD_SIZE), lambda i, _: (0, 0))
+    return pl.pallas_call(
+        functools.partial(attend_kernel, span),
+        out_shape=jax.ShapeDtypeStruct((slot_total * span, q_width), jnp.bfloat16),
+        grid_spec=pltpu.PrefetchScalarGridSpec(
+            num_scalar_prefetch=1,
+            grid=(kv_count,),
+            in_specs=[
+                pl.BlockSpec((tokens, per_kv), lambda i, _: (0, i)),
+                pl.BlockSpec((tokens, HEAD_SIZE), lambda i, _: (0, first_key + i)),
+                pl.BlockSpec((tokens, HEAD_SIZE), lambda i, _: (0, first_key + kv_count + i)),
+                pl.BlockSpec((1, per_kv), lambda i, _: (0, i)),
+                pl.BlockSpec((2, HEAD_SIZE), lambda i, _: (0, i)),
+                table,
+                table,
+            ],
+            out_specs=pl.BlockSpec((slot_total * span, per_kv), lambda i, _: (0, i)),
+            scratch_shapes=[pltpu.VMEM((tokens, per_kv), jnp.bfloat16)],
+        ),
+        compiler_params=pltpu.CompilerParams(vmem_limit_bytes=48 * 1024 * 1024),
+        cost_estimate=pl.CostEstimate(
+            flops=4 * tokens * 128 * q_width,
+            bytes_accessed=tokens * q_width * 4 + slot_total * span * q_width * 2,
+            transcendentals=tokens * q_width,
+        ),
+    )(
+        slot_resp, raw, raw, raw, bias_q.reshape(1, q_width), key_value_bias,
+        jnp.asarray(cosine), jnp.asarray(sine_part),
+    )
 
 
 def normalize(blocks, norm_gain):
@@ -289,6 +352,7 @@
                 token_copy(block, piece, False).wait_send()
 
     strip = 16
+    width_x = xbuf.shape[2]
     features = tp_size * xbuf.shape[2]
 
     def normalize_strip(i, carry):
@@ -300,7 +364,7 @@
         scale = lax.rsqrt(squares / features + eps_norm)
         for block in range(tp_size):
             wide = xbuf[block, rows, :].astype(jnp.float32)
-            xbuf[block, rows, :] = (wide * scale * gain_ref[block : block + 1, :]).astype(
+            xbuf[block, rows, :] = (wide * scale * gain_ref[0:1, block * width_x : (block + 1) * width_x]).astype(
                 jnp.bfloat16
             )
         return carry
@@ -382,7 +446,7 @@
             bytes_accessed=tokens * features * 2 + depth * width * 2 + tokens * width * 4,
             transcendentals=0,
         ),
-    )(x, w_q, w_pairs, norm_gain.reshape(tp_size, features))
+    )(x, w_q, w_pairs, norm_gain.reshape(1, tp_size * features))
 
 
 def on_device(
@@ -406,74 +470,85 @@
     nshard = lax.axis_size("fsdp")
     resp_count, resp_span, feature_width = resp_embed.shape
     packed_len = resp_count * resp_span
+    capacity = 2 * resp_count // nshard
+    slot_total = nshard * capacity
+    facts = jnp.concatenate(
+        [resp_ids, resp_lengths[:, None], dest_offset[:, None], dest_shard[:, None]], axis=1
+    )
+    facts = lax.all_gather(facts, "fsdp", axis=0, tiled=True)
+
     own_rows = resp_embed.reshape(packed_len, feature_width)
     pair_width = key_value_weight.shape[1] * key_value_weight.shape[2]
-    kv_width = pair_width // 2
-    kv_count = kv_width // HEAD_SIZE
     w_pairs = key_value_weight.reshape(key_value_weight.shape[0], pair_width)
     q_width = w_q.shape[1]
     if nshard == 8 and w_q.shape[0] * 2 == feature_width:
         raw = gather_project(own_rows, w_q, w_pairs, norm_gain)
-        query_raw, pair_raw = raw[:, :q_width], raw[:, q_width:]
     else:
         normed = normalize(lax.all_gather(own_rows, "tp", axis=0, tiled=False), norm_gain)
         normed = jnp.swapaxes(normed, 0, 1).reshape(packed_len, -1)
-        query_raw, pair_raw = (
-            jnp.dot(
-                normed,
-                lax.all_gather(w, "fsdp", axis=0, tiled=True),
-                preferred_element_type=jnp.float32,
-            )
-            for w in (w_q, w_pairs)
-        )
+        raw = jnp.concatenate(
+            [
+                jnp.dot(
+                    normed,
+                    lax.all_gather(w, "fsdp", axis=0, tiled=True),
+                    preferred_element_type=jnp.float32,
+                )
+                for w in (w_q, w_pairs)
+            ],
+            axis=1,
+        )
+
+    def slots_of(shards):
+        before = jnp.arange(resp_count, dtype=jnp.int32)
+        same = (shards[..., None, :] == shards[..., :, None]) & (
+            before[None, :] < before[:, None]
+        )
+        return jnp.sum(same.astype(jnp.int32), axis=-1)
+
+    own_slot = dest_shard * capacity + slots_of(dest_shard)
+    every_slot = jnp.arange(slot_total, dtype=jnp.int32)
+    slot_resp = jnp.sum(
+        jnp.where(
+            own_slot[:, None] == every_slot[None, :],
+            jnp.arange(resp_count, dtype=jnp.int32)[:, None],
+            0,
+        ),
+        axis=0,
+    )
+    slots = attend_responses(raw, slot_resp, bias_q, key_value_bias, resp_span)
+    slots = slots.reshape(nshard, capacity * resp_span, q_width)
+    arrived = lax.all_to_all(slots, "fsdp", split_axis=0, concat_axis=0, tiled=True)
+    arrived = arrived.reshape(slot_total * resp_span, q_width)
 
     decode_out = decode_local(
         dec_queries, cache_keys, cached_value_rows, step_keys, step_values, prompt_lengths
     )
 
-    capacity = 2 * resp_count // nshard
-    indices = jnp.arange(resp_count, dtype=jnp.int32)
-    earlier = (dest_shard[None, :] == dest_shard[:, None]) & (indices[None, :] < indices[:, None])
-    pair_rank = jnp.sum(earlier.astype(jnp.int32), axis=1)
-    placing = (dest_shard[:, None, None] == jnp.arange(nshard, dtype=jnp.int32)[None, :, None]) & (
-        pair_rank[:, None, None] == jnp.arange(capacity, dtype=jnp.int32)[None, None, :]
-    )
-    facts = jnp.concatenate([resp_ids, resp_lengths[:, None], dest_offset[:, None]], axis=1)
-    slot_facts = jnp.sum(jnp.where(placing[:, :, :, None], facts[:, None, None, :], 0), axis=0)
-    arrived_facts = lax.all_to_all(slot_facts, "fsdp", split_axis=0, concat_axis=0, tiled=True)
-    slot_total = nshard * capacity
-    arrived_facts = arrived_facts.reshape(slot_total, resp_span + 2)
-    ids_in = arrived_facts[:, :resp_span]
-    lengths_in = arrived_facts[:, resp_span]
-    offsets_in = arrived_facts[:, resp_span + 1]
+    shards = facts[:, resp_span + 2]
+    source_slot = (
+        jnp.arange(nshard, dtype=jnp.int32)[:, None] * capacity
+        + slots_of(shards.reshape(nshard, resp_count))
+    ).reshape(nshard * resp_count)
+    mine = shards == lax.axis_index("fsdp")
+    placing = mine[:, None] & (source_slot[:, None] == every_slot[None, :])
+    slot_facts = jnp.sum(
+        jnp.where(placing[:, :, None], facts[:, None, : resp_span + 2], 0), axis=0
+    )
+    ids_in = slot_facts[:, :resp_span]
+    lengths_in = slot_facts[:, resp_span]
+    offsets_in = slot_facts[:, resp_span + 1]
     position = jnp.arange(packed_len, dtype=jnp.int32)
-    picks = (
-        position[:, None, None]
-        == offsets_in[None, :, None] + jnp.arange(resp_span, dtype=jnp.int32)[None, None, :]
-    ) & (jnp.arange(resp_span, dtype=jnp.int32)[None, None, :] < lengths_in[None, :, None])
+    within = jnp.arange(resp_span, dtype=jnp.int32)
+    picks = (position[:, None, None] == offsets_in[None, :, None] + within[None, None, :]) & (
+        within[None, None, :] < lengths_in[None, :, None]
+    )
     picks = picks.reshape(packed_len, slot_total * resp_span)
     packed_ids = jnp.sum(
         jnp.where(picks, ids_in.reshape(1, slot_total * resp_span) + 1, 0), axis=1
     ) - 1
-    picks = picks.astype(jnp.bfloat16)
-
-    table = rotary_table(resp_span)
-    pair_raw = pair_raw.reshape(packed_len, 2, kv_width) + key_value_bias[None]
-    ref_keys = rotate_half(
-        pair_raw[:, 0].reshape(resp_count, resp_span, kv_count, HEAD_SIZE), table
+    ref_attn = jnp.dot(
+        picks.astype(jnp.bfloat16), arrived, preferred_element_type=jnp.float32
     ).astype(jnp.bfloat16)
-    ref_values = (
-        pair_raw[:, 1].reshape(resp_count, resp_span, kv_count, HEAD_SIZE).astype(jnp.bfloat16)
-    )
-    attn = attend_responses(query_raw + bias_q[None, :], ref_keys, ref_values, table)
-    spread = jnp.swapaxes(placing.reshape(resp_count, slot_total), 0, 1).astype(jnp.bfloat16)
-    slots = jnp.einsum(
-        "sk,krx->srx", spread, attn, preferred_element_type=jnp.float32
-    ).astype(jnp.bfloat16)
-    slots = slots.reshape(nshard, capacity * resp_span, q_width)
-    arrived = lax.all_to_all(slots, "fsdp", split_axis=0, concat_axis=0, tiled=True)
-    arrived = arrived.reshape(slot_total * resp_span, q_width)
-    ref_attn = jnp.dot(picks, arrived, preferred_element_type=jnp.float32).astype(jnp.bfloat16)
     return (decode_out, packed_ids, ref_attn)
 
 

time: 291 us -> 272 us (0.935)
  blocking collectives: 0 us -> 32.2 us
  waiting for transfers between devices: 26.2 us -> 0.01 us
  local copies, waits for them, and re-layouts: 36.4 us -> 20.1 us
  Pallas kernels: 189 us -> 198 us
  matrix products: 17.7 us -> 10.6 us
  other arithmetic: 10 us -> 4.53 us
  starting transfers between devices: 9.86 us -> 4.68 us
    all_gather x0 -> x1, blocking collectives: none -> 32.2 us  [on_device(): facts = lax.all_gather(facts, 'fsdp', axis=0, tiled=True)]
    all_to_all x1, waiting for transfers between devices: 26.2 us -> 0.01 us  [on_device(): lax.all_to_all(slots, 'fsdp', split_axis=0, concat_axis=0, tiled=True)]
    pallas_call x0 -> x1, Pallas kernels: none -> 9.18 us  [attend_responses(): pl.pallas_call(functools.partial(attend_kernel, span), out_shape=jax.Shap...]
    convert_element_type x4 -> x0, local copies, waits for them, and re-layouts: 7.44 us -> none  [the longest x1 4.27 us: on_device(): slots = jnp.einsum('sk,krx->srx', spread, attn, preferred_element_type=jn...]
    dot_general x4 -> x1, matrix products: 12.9 us -> 5.84 us  [on_device(): jnp.dot(picks.astype(jnp.bfloat16), arrived, preferred_element_type=jnp.f...]
    all_to_all x1 -> x0, starting transfers between devices: 5.17 us -> none  [on_device(): lax.all_to_all(slot_facts, 'fsdp', split_axis=0, concat_axis=0, tiled=True)]
    another operation x2 -> x0, other arithmetic: 2.98 us -> none
    another operation x3 -> x0, local copies, waits for them, and re-layouts: 2.95 us -> none
  transfers between devices with their start and end apart: 2 -> 1, of which waited for: 1 -> 0; matrix products, arithmetic and copies ran while one was open for 18% -> 9% of each run, Pallas kernels for 65% -> 0%
where the time goes in v3:
time: 272 us; the launch traced here: 271 us
  Pallas kernels  198 us (73%)
  blocking collectives  32.2 us (12%)
  local copies, waits for them, and re-layouts  20.1 us (7%)
  matrix products  10.6 us (4%)
  starting transfers between devices  4.68 us (2%)
  other arithmetic  4.53 us (2%)
    pallas_call x1, Pallas kernels, gather_project(): pl.pallas_call(gather_project_kernel, out_shape=jax.ShapeDtypeStruct((tok...  189 us
    all_gather x1, blocking collectives, on_device(): facts = lax.all_gather(facts, 'fsdp', axis=0, tiled=True)  32.2 us
    pallas_call x1, Pallas kernels, attend_responses(): pl.pallas_call(functools.partial(attend_kernel, span), out_shape=jax.Shap...  9.18 us
    reshape x1, local copies, waits for them, and re-layouts, decode_local(): key_matrix = cache_keys.reshape(row_count, length, kv_local, HEAD_SIZE)  6.94 us
    reshape x1, local copies, waits for them, and re-layouts, decode_local(): cached_value_rows.reshape(row_count, length, kv_local, HEAD_SIZE)  6.91 us
    dot_general x1, matrix products, on_device(): jnp.dot(picks.astype(jnp.bfloat16), arrived, preferred_element_type=jnp.f...  5.84 us
  transfers between devices with their start and end apart: 1, of which 0 were waited for; matrix products, arithmetic and copies ran while one was open for 9% of the time, Pallas kernels for 0%

profile of v3, /device:TPU:0, one launch (start us, length us, event | category | flops | bytes accessed | tf_op | source)
XLA Modules:
  0.0 271.4 jit_solution(1470302950662251031)
XLA Ops:
  0.6 2.4 copy.74
  3.1 0.9 convert_reduce_fusion.1
  4.0 0.7 multiply_add_fusion
  4.6 0.1 select_reduce_fusion.2.slot_resp
  4.7 0.0 copy-start.1
  4.7 0.0 copy-start.2
  4.7 0.0 copy-start.3
  4.7 0.0 copy-start.4
  4.8 189.1 %shard_map.193.q_ref.k_ref.v_ref = f32[512,2560]{1,0:T(8,128)} custom-call(bf16[512,2048]{1,0:T(8,128)(2,1)} %bitcast.42, bf16[1024,2048]{1,0:T(8,128)(2,1)} %wq_ref.1, bf16[1024,512]{1,0:T(8,128)(2,1)} %bitcast.35, f32[1,8192]{1,0:T(1,128)} %bitcast.43), custom_call_target="tpu_custom_call" | custom-call | flops 21474836480 | bytes 12582912 | tf_op jit(solution)/shard_map/pallas_call | solution.py:422
  193.9 0.0 copy-done.1
  193.9 0.0 copy-done.2
  193.9 0.0 copy-done.3
  193.9 0.0 copy-done.4
  193.9 9.2 %shard_map.194 = bf16[1024,2048]{1,0:T(8,128)(2,1)S(1)} custom-call(s32[32]{0:T(128)S(1)} %select_reduce_fusion.2.slot_resp, f32[512,2560]{1,0:T(8,128)} %shard_map.193.q_ref.k_ref.v_ref, f32[512,2560]{1,0:T(8,128)} %shard_map.193.q_ref.k_ref.v_ref, f32[512,2560]{1,0:T(8,128)} %shard_map.193.q_ref.k_ref.v_ref, f32[1,2048]{1,0:T(1,128)S(1)} %bitcast.31, ...), custom_call_target="tpu_custom_call" | custom-call | flops 536870912 | bytes 8388608 | tf_op jit(solution)/shard_map/pallas_call | solution.py:130
  203.1 0.0 copy-start
  203.1 2.0 copy-done
  205.1 0.0 copy-start.6
  205.1 0.0 copy-start.10
  205.1 0.0 copy-start.8
  205.1 4.7 %all-to-all-start = ((bf16[8,128,2048]{2,1,0:T(8,128)(2,1)}), bf16[8,128,2048]{2,1,0:T(8,128)(2,1)}, u32[]{:S(2)}, u32[]{:S(2)}) async-start(bf16[8,128,2048]{2,1,0:T(8,128)(2,1)} %bitcast.30), calls=%async_computation | async-start | bytes 8388608 | tf_op jit(solution)/shard_map/all_to_all | solution.py:520
  209.8 0.0 copy-done.6
  209.8 0.0 copy-done.10
  209.8 0.1 iota_compare_fusion.1
  209.9 0.0 copy-done.8
  209.9 0.2 fusion.33
  210.2 0.0 copy-start.9
  210.2 6.9 %reshape.218 = bf16[2,4096,2,128]{3,2,1,0:T(2,128)(2,1)} reshape(bf16[2,4096,256]{2,1,0:T(8,128)(2,1)} %param.19) | data formatting | bytes 8388608 | tf_op jit(solution)/shard_map/reshape | solution.py:29
  217.1 0.0 copy-done.9
  217.1 6.9 %reshape.221 = bf16[2,4096,2,128]{3,2,1,0:T(2,128)(2,1)} reshape(bf16[2,4096,256]{2,1,0:T(8,128)(2,1)} %param.20) | data formatting | bytes 8388608 | tf_op jit(solution)/shard_map/reshape | solution.py:30
  224.0 3.6 %fusion.32 = (f32[2,2,2,8]{3,0,2,1:T(2,128)S(1)}, f32[2,2,2,8,4096]{4,3,0,2,1:T(8,128)S(1)}) fusion(bf16[2,2,2,8,128]{4,3,2,1,0:T(8,128)(2,1)S(1)} %reshape.219, bf16[2,4096,2,128,1]{3,2,1,0,4:T(2,128)(2,1)} %bitcast.33, pred[2,4096]{1,0:T(4,128)(4,1)S(1)} %iota_compare_fusion.1), kind=kOutput, calls=%fused_computation.55 | convolution fusion | flops 67895232 | bytes 5267712 | tf_op jit(solution)/shard_map/srkgd,rckd->srkgc/dot_general | solution.py:34
  227.7 0.3 fusion.20
  228.0 0.2 fusion.27
  228.2 0.0 copy-done.5
  228.2 0.0 copy-start.13
  228.2 0.0 copy-start.7
  228.3 0.7 fusion.13
  229.0 0.6 convert_element_type.29
  229.6 0.0 copy-done.11
  229.6 0.1 copy.57
  229.7 0.0 copy-done.12
  229.7 0.1 copy.58
  229.8 0.0 copy-done.13
  229.8 0.1 copy.59
  229.9 0.0 copy-done.7
  229.9 0.1 pad_add_fusion
  230.0 32.2 %all_gather.3 = s32[128,35]{1,0:T(8,128)S(1)} all-gather(s32[16,35]{1,0:T(8,128)S(1)} %pad_add_fusion), channel_id=1, replica_groups=mesh['fsdp'=8,'tp'=4] {'fsdp'}, dimensions={0}, use_global_device_ids=true | all-gather | bytes 20160 | tf_op jit(solution)/shard_map/all_gather | solution.py:478
  262.2 0.2 slice_reduce_fusion
  262.4 0.1 eq.85
  262.5 0.3 convert_reduce_fusion
  262.8 0.1 broadcast_add_fusion
  262.8 0.1 add.75
  262.9 0.1 copy.60
  263.0 0.2 compare_reduce_fusion
  263.2 0.7 select_reduce_fusion.1
  263.9 0.2 broadcast_reduce_fusion
  264.1 0.1 add.77
  264.1 0.1 add.79
  264.2 0.1 lt.72
  264.3 0.1 copy.61
  264.4 0.1 add.83
  264.5 0.5 select_reduce_fusion
  265.0 0.6 broadcast_add_fusion.1
  265.5 0.0 all-to-all-done
  265.5 5.8 %convolution_convert_fusion = bf16[512,2048]{1,0:T(8,128)(2,1)} fusion(bf16[1024,2048]{1,0:T(8,128)(2,1)} %bitcast.16, s32[1024]{0:T(1024)S(1)} %add.80, pred[1024]{0:T(1024)(128)(4,1)S(1)} %lt.73), kind=kOutput, calls=%fused_computation.6 | convolution fusion | flops 2149580800 | bytes 6296576 | tf_op jit(solution)/shard_map/dot_general | solution.py:549
  (19 shorter events, 0.2 us)
Async XLA Ops:
  4.7 189.2 %copy-start.1 = (f32[32,128]{1,0:T(8,128)S(1)}, f32[32,128]{1,0:T(8,128)}, u32[]{:S(2)}) copy-start(f32[32,128]{1,0:T(8,128)} %constant.27.clone.cos_ref) | copy-start | bytes 49156
  4.7 189.2 %copy-start.2 = (f32[32,128]{1,0:T(8,128)S(1)}, f32[32,128]{1,0:T(8,128)}, u32[]{:S(2)}) copy-start(f32[32,128]{1,0:T(8,128)} %constant.28.clone.sin_ref) | copy-start | bytes 49156
  4.7 189.2 %copy-start.3 = (f32[2048]{0:T(1024)S(1)}, f32[2048]{0:T(1024)}, u32[]{:S(2)}) copy-start(f32[2048]{0:T(1024)} %param.32) | copy-start | bytes 24580
  4.7 189.2 %copy-start.4 = (f32[2,256]{1,0:T(2,128)S(1)}, f32[2,256]{1,0:T(2,128)}, u32[]{:S(2)}) copy-start(f32[2,256]{1,0:T(2,128)} %bias_kv_ref.1) | copy-start | bytes 6148
  203.1 2.0 copy-start
  205.1 4.7 %copy-start.6 = (bf16[2,2,2048]{2,1,0:T(2,128)(2,1)S(1)}, bf16[2,2,2048]{2,1,0:T(2,128)(2,1)}, u32[]{:S(2)}) copy-start(bf16[2,2,2048]{2,1,0:T(2,128)(2,1)} %param.18) | copy-start | bytes 49156
  205.1 4.7 %copy-start.10 = (s32[2]{0:T(128)S(1)}, s32[2]{0:T(128)}, u32[]{:S(2)}) copy-start(s32[2]{0:T(128)} %param.23) | copy-start | bytes 28
  205.1 4.8 %copy-start.8 = (bf16[2,2,256]{2,1,0:T(2,128)(2,1)S(1)}, bf16[2,2,256]{2,1,0:T(2,128)(2,1)}, u32[]{:S(2)}) copy-start(bf16[2,2,256]{2,1,0:T(2,128)(2,1)} %param.21) | copy-start | bytes 6148
  205.1 60.5 %all-to-all-start = ((bf16[8,128,2048]{2,1,0:T(8,128)(2,1)}), bf16[8,128,2048]{2,1,0:T(8,128)(2,1)}, u32[]{:S(2)}, u32[]{:S(2)}) async-start(bf16[8,128,2048]{2,1,0:T(8,128)(2,1)} %bitcast.30), calls=%async_computation | async-start | bytes 8388608 | tf_op jit(solution)/shard_map/all_to_all | solution.py:520
  210.2 7.0 %copy-start.9 = (bf16[2,2,256]{2,1,0:T(2,128)(2,1)S(1)}, bf16[2,2,256]{2,1,0:T(2,128)(2,1)}, u32[]{:S(2)}) copy-start(bf16[2,2,256]{2,1,0:T(2,128)(2,1)} %param.22) | copy-start | bytes 6148
  224.0 4.2 %copy-start.5 = (bf16[2,4096,2,128]{3,2,1,0:T(2,128)(2,1)S(1)}, bf16[2,4096,2,128]{3,2,1,0:T(2,128)(2,1)}, u32[]{:S(2)}) copy-start(bf16[2,4096,2,128]{3,2,1,0:T(2,128)(2,1)} %reshape.221) | copy-start | bytes 12582916
  228.2 1.4 copy-start.11
  228.2 1.5 copy-start.12
  228.2 1.6 copy-start.13
  228.2 1.7 copy-start.7
